TPU v7x, 256 devices: a whole 4x4x8 slice. The times are simulated.
256 devices in a mesh: dp: 64 (over z, x, core), mp: 4 (over y).
Axes of the slice: x: 4, y: 4, z: 8, core: 2. Of those that a mesh axis runs over, the one named last changes fastest.
Arguments:
- query_text_memory: bfloat16 [2, 64, 64, 4096], P(None, 'dp', None, 'mp'), may hold values from -1.5 to 1.5
- query_text_feed: bfloat16 [64, 64, 4096], P('dp', None, 'mp'), may hold values from -6 to 6
- reply_acceptor_memory: bfloat16 [3, 128, 64, 4096], P(None, 'dp', None, 'mp'), may hold values from -1.5 to 1.5
- reply_feed: bfloat16 [128, 64, 4096], P('dp', None, 'mp'), may hold values from -6 to 6
- reply_cotangent_vector: bfloat16 [128, 64, 4096], P('dp', None, 'mp'), may hold values from -6 to 6
- query_placement: int32 [64], replicated, may hold values from 0 to 63, each once
- reply_parent_query: int32 [128], replicated, may hold values from 0 to 63, as said below
- fading_narrowing: float32 [4096, 128], P('mp'), may hold values from -0.09375 to 0.09375
- fading_widening: float32 [128, 4096], P(None, 'mp'), may hold values from -0.5 to 0.5
- fading_anchor_rate: float32 [4096], P('mp'), may hold values from -8 to -2
- self_emphasis: float32 [4096], P('mp'), may hold values from 0.2 to 1.5
- lagged_token_fraction: float32 [4096], P('mp'), may hold values from 0.05 to 0.95
Outputs:
- response_rkv_grad: bfloat16 [3, 128, 64, 4096], P(None, 'dp', None, 'mp')
- response_x_grad: bfloat16 [128, 64, 4096], P('dp', None, 'mp')
- prompt_kv_grad: bfloat16 [2, 64, 64, 4096], P(None, 'dp', None, 'mp')
- prompt_x_grad: bfloat16 [64, 64, 4096], P('dp', None, 'mp')
- lora_down_grad: float32 [4096, 128], P('mp')
- lora_up_grad: float32 [128, 4096], P(None, 'mp')
- decay_base_grad: float32 [4096], P('mp')
- self_emphasis_adjoint: float32 [4096], P('mp')
- shift_mix_grad: float32 [4096], P('mp')
Inputs may be any that keep to these rules, and one draw needn't show every extreme that they name: `reply_parent_query`: each prompt is named by exactly 2 responses.
All inputs are finite; a program needn't handle non-finite values.
Results may differ from a plain program's by a relative error of at most 0.0015.
Values sent between devices are 32-bit elements; how exact they have to be, the bound alone decides.
A program may use at most 128 MiB of HBM per device.

v0:
```python
import jax
import jax.numpy as jnp
from jax import lax
from jax.sharding import PartitionSpec as P

CHANNEL_COUNT = 64
BLK = 16


highest_precision = lax.Precision.HIGHEST


def mixing_input(input_rows, leading_row, lagged_token_fraction, fading_narrowing):
    previous = jnp.concatenate([leading_row[None, :], input_rows[:-1]], axis=0)
    mixed_input = input_rows + (previous - input_rows) * lagged_token_fraction
    return jnp.dot(
        mixed_input,
        fading_narrowing,
        precision=highest_precision,
        preferred_element_type=jnp.float32,
    )


def decay_row_values(hidden_entries, fading_widening, fading_anchor_rate):
    return -jnp.exp(
        fading_anchor_rate
        + jnp.dot(
            jnp.tanh(hidden_entries),
            fading_widening,
            precision=highest_precision,
            preferred_element_type=jnp.float32,
        )
    )


def segment_summands(memory_amount, element_sequence, self_emphasis_grouped):
    acceptor_entries, address_entries, values, log_rows = element_sequence
    cumulative = jnp.cumsum(log_rows, axis=0)
    before = cumulative - log_rows
    count = address_entries.shape[0]
    earlier = (jnp.arange(count)[:, None] > jnp.arange(count)[None, :])[:, :, None, None]
    log_gap = jnp.where(earlier, before[:, None] - cumulative[None, :], 0.0)
    decay = jnp.where(earlier, jnp.exp(log_gap), 0.0)
    scores = jnp.einsum(
        "thc,shc,tshc->hts", acceptor_entries, address_entries, decay, precision=highest_precision
    )
    self_token_addend = jnp.sum(acceptor_entries * self_emphasis_grouped * address_entries, axis=2)
    output_rows = (
        jnp.einsum("hts,shd->thd", scores, values, precision=highest_precision)
        + self_token_addend[:, :, None] * values
    )
    output_rows = output_rows + jnp.einsum(
        "thc,hcd->thd",
        acceptor_entries * jnp.exp(before),
        memory_amount,
        precision=highest_precision,
    )
    block_end = cumulative[-1]
    memory_amount = jnp.exp(block_end)[:, :, None] * memory_amount + jnp.einsum(
        "shc,shd->hcd",
        address_entries * jnp.exp(block_end[None] - cumulative),
        values,
        precision=highest_precision,
    )
    return (memory_amount, output_rows)


def reply_entries_group(
    hidden_entries,
    opening_amount,
    threefold_bundle,
    fading_widening,
    fading_anchor_rate,
    self_emphasis,
):
    log_values = decay_row_values(hidden_entries, fading_widening, fading_anchor_rate)
    length, channels = log_values.shape
    channel_groups = channels // CHANNEL_COUNT
    shape = (length // BLK, BLK, channel_groups, CHANNEL_COUNT)
    self_emphasis_grouped = self_emphasis.reshape(channel_groups, CHANNEL_COUNT)

    def reply_advance(memory_amount, element_sequence):
        return segment_summands(memory_amount, element_sequence, self_emphasis_grouped)

    ending, output_rows = lax.scan(
        jax.checkpoint(reply_advance),
        opening_amount,
        (
            threefold_bundle[0].reshape(shape),
            threefold_bundle[1].reshape(shape),
            threefold_bundle[2].reshape(shape),
            log_values.reshape(shape),
        ),
    )
    return output_rows.reshape(length, channels)


def prompt_recurrence_core(hidden_entries, pair_tuple, fading_widening, fading_anchor_rate):
    log_values = decay_row_values(hidden_entries, fading_widening, fading_anchor_rate)
    length, channels = log_values.shape
    channel_groups = channels // CHANNEL_COUNT
    shape = (length // BLK, BLK, channel_groups, CHANNEL_COUNT)

    def prompt_advance(memory_amount, element_sequence):
        address_entries, values, log_rows = element_sequence
        cumulative = jnp.cumsum(log_rows, axis=0)
        block_end = cumulative[-1]
        carried = jnp.exp(block_end)[:, :, None] * memory_amount
        return (
            carried
            + jnp.einsum(
                "shc,shd->hcd",
                address_entries * jnp.exp(block_end[None] - cumulative),
                values,
                precision=highest_precision,
            ),
            None,
        )

    opening_amount = jnp.zeros((channel_groups, CHANNEL_COUNT, CHANNEL_COUNT), jnp.float32)
    memory_amount, unused = lax.scan(
        jax.checkpoint(prompt_advance),
        opening_amount,
        (pair_tuple[0].reshape(shape), pair_tuple[1].reshape(shape), log_values.reshape(shape)),
    )
    return memory_amount


def decay_factor_total(partial_row_block):
    return lax.psum(partial_row_block, "mp")


def return_pieces(parts):
    return (
        lax.all_to_all(parts[0], "dp", split_axis=1, concat_axis=1, tiled=True),
        lax.all_to_all(parts[1], "dp", split_axis=1, concat_axis=1, tiled=True),
    )


def per_device(
    query_text_memory,
    query_text_feed,
    reply_acceptor_memory,
    reply_feed,
    reply_cotangent_vector,
    query_placement,
    reply_parent_query,
    fading_narrowing,
    fading_widening,
    fading_anchor_rate,
    self_emphasis,
    lagged_token_fraction,
):
    devices = lax.axis_size("dp")
    position = lax.axis_index("dp")
    slots = reply_acceptor_memory.shape[1]
    channels = query_text_feed.shape[2]
    channel_groups = channels // CHANNEL_COUNT
    width = channels * CHANNEL_COUNT
    matches = (query_placement[None, :] == reply_parent_query[:, None]).astype(jnp.int32)
    owner = jnp.sum(jnp.arange(devices, dtype=jnp.int32)[None, :] * matches, axis=1)
    by_device = owner.reshape(devices, slots)
    my_owners = lax.dynamic_slice_in_dim(owner, position * slots, slots)
    couple_segment = query_text_memory[:, 0].astype(jnp.float32)
    query_segment = query_text_feed[0].astype(jnp.float32)
    blank_row = jnp.zeros((channels,), jnp.float32)

    def prompt_mixing(rows, blend_coeffs, narrowing_grid):
        return mixing_input(rows, blank_row, blend_coeffs, narrowing_grid)

    prompt_portion, prompt_mixing_backward = jax.vjp(
        prompt_mixing, query_segment, lagged_token_fraction, fading_narrowing
    )
    prompt_activation = decay_factor_total(prompt_portion)
    final_state, prompt_core_backward = jax.vjp(
        prompt_recurrence_core,
        prompt_activation,
        couple_segment,
        fading_widening,
        fading_anchor_rate,
    )
    flat_state = final_state.reshape(1, width)
    last_row = query_segment[-1].reshape(1, channels)
    piece = (
        lax.all_gather(flat_state, "dp", axis=0, tiled=True),
        lax.all_gather(last_row, "dp", axis=0, tiled=True),
    )
    rows = jnp.arange(piece[0].shape[0])
    selector = (my_owners[:, None] == rows[None, :]).astype(jnp.float32)
    start_flat = jnp.dot(selector, piece[0], precision=highest_precision)
    leading_rows = jnp.dot(selector, piece[1], precision=highest_precision)
    start_values = start_flat.reshape(slots, channel_groups, CHANNEL_COUNT, CHANNEL_COUNT)
    threefold_bundle = reply_acceptor_memory.astype(jnp.float32)
    reply_segment = reply_feed.astype(jnp.float32)

    def response_mixing(firsts, rows, blend_coeffs, narrowing_grid):
        return jax.vmap(mixing_input, in_axes=(0, 0, None, None))(
            rows, firsts, blend_coeffs, narrowing_grid
        )

    def response_complete(
        hidden_entries,
        opening_memories,
        threefold_group,
        widening_grid,
        fading_anchor_coeffs,
        self_emphasis_grid,
    ):
        return jax.vmap(reply_entries_group, in_axes=(0, 0, 1, None, None, None))(
            hidden_entries,
            opening_memories,
            threefold_group,
            widening_grid,
            fading_anchor_coeffs,
            self_emphasis_grid,
        )

    response_portion, response_mix_back = jax.vjp(
        response_mixing, leading_rows, reply_segment, lagged_token_fraction, fading_narrowing
    )
    response_activation = decay_factor_total(response_portion)
    emitted_results, response_backward = jax.vjp(
        response_complete,
        response_activation,
        start_values,
        threefold_bundle,
        fading_widening,
        fading_anchor_rate,
        self_emphasis,
    )
    (
        activation_gradient,
        start_gradient,
        triple_gradient,
        up_gradient,
        decay_base_gradient,
        self_emphasis_adjoint,
    ) = response_backward(reply_cotangent_vector.astype(jnp.float32))
    activation_gradient = decay_factor_total(activation_gradient)
    first_grad, rows_grad, mix_grad, down_grad = response_mix_back(activation_gradient)
    pieces_states, pieces_rows = return_pieces(
        (start_gradient.reshape(slots, devices, -1), first_grad.reshape(slots, devices, -1))
    )
    owner_rows = by_device.T.reshape(-1)
    selector = (jnp.arange(devices)[:, None] == owner_rows[None, :]).astype(jnp.float32)
    summed_states = jnp.dot(
        selector, pieces_states.reshape(slots * devices, -1), precision=highest_precision
    )
    summed_rows = jnp.dot(
        selector, pieces_rows.reshape(slots * devices, -1), precision=highest_precision
    )
    home_states, home_rows = return_pieces((summed_states[None], summed_rows[None]))
    prompt_activation_gradient, pair_grad, up_grad_prompt, base_grad_prompt = prompt_core_backward(
        home_states.reshape(channel_groups, CHANNEL_COUNT, CHANNEL_COUNT)
    )
    prompt_activation_gradient = decay_factor_total(prompt_activation_gradient)
    prompt_rows_grad, mix_grad_prompt, down_grad_prompt = prompt_mixing_backward(
        prompt_activation_gradient
    )
    prompt_rows_grad = prompt_rows_grad.at[-1].add(home_rows.reshape(channels))
    totals = lax.psum(
        (
            down_grad + down_grad_prompt,
            up_gradient + up_grad_prompt,
            decay_base_gradient + base_grad_prompt,
            self_emphasis_adjoint,
            mix_grad + mix_grad_prompt,
        ),
        "dp",
    )
    return (
        triple_gradient.astype(jnp.bfloat16),
        rows_grad.astype(jnp.bfloat16),
        pair_grad[:, None].astype(jnp.bfloat16),
        prompt_rows_grad[None].astype(jnp.bfloat16),
        totals[0],
        totals[1],
        totals[2],
        totals[3],
        totals[4],
    )


def solution(mesh):
    in_specs = (
        P(None, "dp", None, "mp"),
        P("dp", None, "mp"),
        P(None, "dp", None, "mp"),
        P("dp", None, "mp"),
        P("dp", None, "mp"),
        P(),
        P(),
        P("mp", None),
        P(None, "mp"),
        P("mp"),
        P("mp"),
        P("mp"),
    )
    out_specs = (
        P(None, "dp", None, "mp"),
        P("dp", None, "mp"),
        P(None, "dp", None, "mp"),
        P("dp", None, "mp"),
        P("mp", None),
        P(None, "mp"),
        P("mp"),
        P("mp"),
        P("mp"),
    )
    return jax.shard_map(
        per_device, mesh=mesh, in_specs=in_specs, out_specs=out_specs, check_vma=False
    )
```

profile of v0, /device:TPU:1, one launch (start us, length us, event | category | flops | bytes accessed | tf_op | source)
XLA Modules:
  0.0 811.5 jit_solution(4792982089442057530)
XLA Ops:
  8.9 48.6 %all-gather = f32[64,1,1024]{2,1,0:T(1,128)S(1)} all-gather(f32[1,1,1024]{2,1,0:T(1,128)S(1)} %slice.93), channel_id=2, replica_groups=mesh['dp'=64,'mp'=4] {'dp'}, dimensions={0}, use_global_device_ids=true | all-gather | bytes 266240 | tf_op jit(solution)/shard_map/all_gather | solution.py:186
  60.4 2.5 fusion.63
  66.1 13.7 %psum.63 = f32[64,128]{1,0:T(8,128)S(1)} all-reduce(f32[64,128]{1,0:T(8,128)S(1)} %fusion.68), channel_id=1, replica_groups=mesh['dp'=64,'mp'=4] {'mp'}, use_global_device_ids=true, to_apply=%region_1.0 | all-reduce | flops 8192 | bytes 65536 | tf_op jit(solution)/shard_map/psum | solution.py:130
  81.6 9.1 %while.73 = (s32[]{:T(128)}, f32[16,64,64]{2,1,0:T(8,128)S(1)}, f32[4,16,64,64]{3,2,1,0:T(8,128)}, f32[4,16,16,64]{3,2,1,0:T(8,128)S(1)}, f32[4,16,16,64]{3,2,1,...) while((s32[]{:T(128)}, f32[16,64,64]{2,1,0:T(8,128)S(1)}, ...), condition=%wide.region_4.5_spmd.clone, body=%wide.region_2.4_spmd.clone.sunk | while | flops 13123587 | bytes 2257516 | solution.py:121
  92.1 2.1 fusion.89
  97.0 2.3 transpose.181
  100.6 2.3 reshape.261
  104.4 2.3 fusion.92
  109.3 82.1 %all-gather.4.cloned.1.call-done = f32[64,1,65536]{2,1,0:T(1,128)} async-done(((f32[1,1,65536]{2,1,0:T(1,128)}), f32[64,1,65536]{2,1,0:T(1,128)}) %all-gather.4.cloned.1.call-update) | async-done | bytes 16777232 | tf_op jit(solution)/shard_map/all_gather | solution.py:185
  191.4 20.9 %fusion.54 = f32[2,65536]{1,0:T(2,128)} fusion(f32[64,1,65536]{2,1,0:T(1,128)} %all-gather.4.cloned.1.call-done, s32[2]{0:T(128)S(1)} %dynamic_slice.115), kind=kOutput, calls=%fused_computation.119 | convolution fusion | flops 100663424 | bytes 17301512 | tf_op jit(solution)/shard_map/dot_general | solution.py:190
  212.3 1.7 reshape.244
  214.0 22.2 %while.71 = (s32[]{:T(128)}, f32[2,16,64,64]{3,2,1,0:T(8,128)S(1)}, f32[4,2,16,64,64]{4,3,2,1,0:T(8,128)}, f32[4,2,16,16,64]{4,3,2,0,1:T(8,128)}, f32[4,2,16,16,...) while((s32[]{:T(128)}, f32[2,16,64,64]{3,2,1,0:T(8,128)S(1)}, ...), condition=%wide.region_8.9_spmd, body=%wide.region_6.8_spmd.sunk | while | flops 25985024 | bytes 4514901 | solution.py:85
  217.1 2.4 convolution_add_fusion.10
  222.7 2.4 convolution_add_fusion.10
  228.2 2.4 convolution_add_fusion.10
  233.8 2.4 convolution_add_fusion.10
  240.5 119.0 %while.74 = (s32[]{:T(128)}, f32[16,64]{1,0:T(8,128)S(1)}, f32[2,16,64,64]{3,2,1,0:T(8,128)}, f32[4,2,16,16,64]{4,2,3,1,0:T(8,128)}, f32[4,2,16,16,64]{4,2,3,1,0...) while((s32[]{:T(128)}, f32[16,64]{1,0:T(8,128)S(1)}, ...), condition=%wide.region_19.20_spmd.clone, body=%wide.region_9.19_spmd.clone.sunk | while | flops 130180416 | bytes 22371852 | solution.py:85
  249.7 1.8 fusion.184
  255.0 2.9 fusion.187
  257.9 1.9 fusion.186
  260.3 3.0 fusion.185
  263.3 1.8 add_add_fusion.2
  266.5 3.0 convolution_add_fusion.12
  279.7 1.8 fusion.184
  285.0 2.9 fusion.187
  287.8 1.9 fusion.186
  290.3 3.0 fusion.185
  293.3 1.8 add_add_fusion.2
  296.4 3.0 convolution_add_fusion.12
  309.6 1.8 fusion.184
  315.0 2.9 fusion.187
  317.8 1.9 fusion.186
  320.3 3.0 fusion.185
  323.3 1.8 add_add_fusion.2
  326.4 3.0 convolution_add_fusion.12
  339.6 1.8 fusion.184
  344.9 2.9 fusion.187
  347.8 1.9 fusion.186
  350.3 3.0 fusion.185
  353.2 1.8 add_add_fusion.2
  356.4 3.0 convolution_add_fusion.12
  365.1 40.7 %all-reduce.18.cloned.1.call-done = f32[2,64,128]{2,1,0:T(8,128)} async-done(((f32[2,64,128]{2,1,0:T(8,128)}), f32[2,64,128]{2,1,0:T(8,128)}) %all-reduce.18.cloned.1.call-update) | async-done | bytes 65552 | tf_op jit(solution)/shard_map/psum | solution.py:130
  405.8 2.2 broadcast_multiply_fusion.1
  409.7 12.7 %all-to-all-start.2 = ((f32[2,64,16]{2,0,1:T(2,128)}), f32[2,64,16]{2,0,1:T(2,128)S(1)}, u32[]{:S(2)}, u32[]{:S(2)}) async-start(f32[2,64,16]{2,0,1:T(2,128)} %copy.188), calls=%async_computation.2 | async-start | bytes 131072 | tf_op jit(solution)/shard_map/all_to_all | solution.py:136
  423.4 2.2 copy.180
  425.7 6.7 all-to-all-done.2
  432.4 5.2 all-to-all-start
  438.0 2.5 copy.175
  440.6 2.3 reshape.248
  442.9 2.5 copy.176
  445.4 2.3 reshape.249
  449.1 2.3 reshape.250
  455.4 9.7 %all-to-all-start.3 = ((f32[1,64,16]{2,0,1:T(1,128)}), f32[1,64,16]{2,0,1:T(1,128)S(1)}, u32[]{:S(2)}, u32[]{:S(2)}) async-start(f32[1,64,16]{2,0,1:T(1,128)} %bitcast.87), calls=%async_computation.3 | async-start | bytes 65536 | tf_op jit(solution)/shard_map/all_to_all | solution.py:136
  467.7 6.8 all-to-all-done.3
  474.5 5.5 all-to-all-start.1
  480.3 2.4 add_convert_fusion
  486.8 6.4 all-to-all-done.1
  497.4 33.1 %while.72 = (s32[]{:T(128)}, f32[16,64,64]{2,1,0:T(8,128)S(1)}, f32[4,16,16,64]{3,2,1,0:T(8,128)}, f32[4,16,16,64]{3,2,1,0:T(8,128)}, f32[4,16,16,64]{3,2,1,0:T(...) while((s32[]{:T(128)}, f32[16,64,64]{2,1,0:T(8,128)S(1)}, ...), condition=%wide.region_26.27_spmd, body=%wide.region_21.26_spmd.sunk | while | flops 26001412 | bytes 3924113 | solution.py:121
  530.5 1.9 neg.63
  534.3 12.1 %psum.66 = f32[64,128]{1,0:T(8,128)S(1)} all-reduce(f32[64,128]{1,0:T(8,128)S(1)} %convolution_multiply_fusion.1), channel_id=1, replica_groups=mesh['dp'=64,'mp'=4] {'mp'}, use_global_device_ids=true, to_apply=%region_27.28 | all-reduce | flops 8192 | bytes 65536 | tf_op jit(solution)/shard_map/psum | solution.py:130
  549.2 1.8 convolution_add_fusion.4
  554.4 244.7 %all-reduce.10 = (f32[1024]{0:T(1024)}, f32[1024]{0:T(1024)}, f32[1024]{0:T(1024)}) all-reduce(f32[1024]{0:T(1024)S(1)} %add.144, f32[1024]{0:T(1024)S(1)} %reshape.260, f32[1024]{0:T(1024)S(1)} %add.145), channel_id=1, replica_groups=mesh['dp'=64,'mp'=4] {'dp'}, use_global_device_ids=true, to_apply=%region_32.33 | all-reduce | flops 3072 | bytes 24576 | tf_op jit(solution)/shard_map/psum | solution.py:261
  799.8 1.9 copy.387
  801.7 1.9 copy.388
  (375 shorter events, 171.3 us)
Async XLA Ops:
  8.0 71.8 %copy-start = (f32[128,1024]{1,0:T(8,128)S(1)}, f32[128,1024]{1,0:T(8,128)}, u32[]{:S(2)}) copy-start(f32[128,1024]{1,0:T(8,128)} %param.30) | copy-start | bytes 1572868
  8.0 56.7 %copy-start.5 = (f32[1024,128]{1,0:T(8,128)S(1)}, f32[1024,128]{1,0:T(8,128)}, u32[]{:S(2)}) copy-start(f32[1024,128]{1,0:T(8,128)} %param.29) | copy-start | bytes 1572868
  8.0 71.8 %copy-start.29 = (f32[1024]{0:T(1024)S(1)}, f32[1024]{0:T(1024)}, u32[]{:S(2)}) copy-start(f32[1024]{0:T(1024)} %param.31) | copy-start | bytes 12292
  8.0 73.0 %copy-start.22 = (bf16[2,1,64,1024]{3,2,1,0:T(8,128)(2,1)S(1)}, bf16[2,1,64,1024]{3,2,1,0:T(8,128)(2,1)}, u32[]{:S(2)}) copy-start(bf16[2,1,64,1024]{3,2,1,0:T(8,128)(2,1)} %param.22) | copy-start | bytes 786436
  8.1 96.4 %all-reduce.16.cloned.1.call-start = ((), (), s32[]{:S(2)}) async-start(), calls=%async_computation.4 | async-start | bytes 131072 | tf_op jit(solution)/shard_map/psum | solution.py:130
  59.6 0.8 copy-start.7
  63.0 128.4 %all-gather.4.cloned.1.call-start = ((), (), s32[]{:S(2)}) async-start(), calls=%async_computation.6 | async-start | bytes 17039360 | tf_op jit(solution)/shard_map/all_gather | solution.py:185
  64.0 0.7 copy-start.15
  90.7 4.7 copy-start.10
  90.8 8.6 %copy-start.11 = (f32[4,16,16,64]{3,2,1,0:T(8,128)}, f32[4,16,16,64]{3,2,1,0:T(8,128)S(1)}, u32[]{:S(2)}) copy-start(f32[4,16,16,64]{3,2,1,0:T(8,128)S(1)} %get-tuple-element.1340) | copy-start | bytes 786436
  90.8 8.6 %copy-start.12 = (f32[4,16,16,64]{3,2,1,0:T(8,128)}, f32[4,16,16,64]{3,2,1,0:T(8,128)S(1)}, u32[]{:S(2)}) copy-start(f32[4,16,16,64]{3,2,1,0:T(8,128)S(1)} %get-tuple-element.1341) | copy-start | bytes 786436
  92.0 313.8 %all-reduce.18.cloned.1.call-start = ((), (), s32[]{:S(2)}) async-start(), calls=%async_computation.5 | async-start | bytes 131072 | tf_op jit(solution)/shard_map/psum | solution.py:130
  94.2 8.7 %copy-start.30 = (f32[1024]{0:T(1024)S(1)}, f32[1024]{0:T(1024)}, u32[]{:S(2)}) copy-start(f32[1024]{0:T(1024)} %param.32) | copy-start | bytes 12292
  108.0 83.4 %copy-start.4 = (f32[2,4,16,16,64]{4,3,2,1,0:T(8,128)}, f32[2,4,16,16,64]{4,3,2,1,0:T(8,128)S(1)}, u32[]{:S(2)}) copy-start(f32[2,4,16,16,64]{4,3,2,1,0:T(8,128)S(1)} %reshape.245) | copy-start | bytes 1572868
  240.7 1.0 copy-start.2
  265.1 4.4 copy-start.3
  269.5 1.0 copy-start.2
  295.1 4.4 copy-start.3
  299.4 1.0 copy-start.2
  325.0 4.4 copy-start.3
  329.4 1.0 copy-start.2
  355.0 4.4 copy-start.3
  359.6 4.3 copy-start.24
  359.6 46.2 %copy-start.6 = (f32[1024,128]{1,0:T(8,128)S(1)}, f32[1024,128]{1,0:T(8,128)}, u32[]{:S(2)}) copy-start(f32[1024,128]{1,0:T(8,128)} %param.29) | copy-start | bytes 1572868
  359.6 46.2 %copy-start.25 = (f32[1024]{0:T(1024)S(1)}, f32[1024]{0:T(1024)}, u32[]{:S(2)}) copy-start(f32[1024]{0:T(1024)} %param.33) | copy-start | bytes 12292
  361.0 61.3 %copy-start.1 = (f32[2,16,64,64]{3,2,1,0:T(8,128)S(1)}, f32[2,16,64,64]{3,2,1,0:T(8,128)}, u32[]{:S(2)}) copy-start(f32[2,16,64,64]{3,2,1,0:T(8,128)} %get-tuple-element.565) | copy-start | bytes 1572868
  408.1 0.8 copy-start.17
  409.7 22.8 %all-to-all-start.2 = ((f32[2,64,16]{2,0,1:T(2,128)}), f32[2,64,16]{2,0,1:T(2,128)S(1)}, u32[]{:S(2)}, u32[]{:S(2)}) async-start(f32[2,64,16]{2,0,1:T(2,128)} %copy.188), calls=%async_computation.2 | async-start | bytes 131072 | tf_op jit(solution)/shard_map/all_to_all | solution.py:136
  425.7 22.1 %copy-start.14 = (f32[4,2,16,16,64]{4,2,3,1,0:T(8,128)S(1)}, f32[4,2,16,16,64]{4,2,3,1,0:T(8,128)}, u32[]{:S(2)}) copy-start(f32[4,2,16,16,64]{4,2,3,1,0:T(8,128)} %get-tuple-element.563) | copy-start | bytes 1572868
  432.4 15.3 %copy-start.26 = (f32[2,64,16]{2,0,1:T(2,128)}, f32[2,64,16]{2,0,1:T(2,128)S(1)}, u32[]{:S(2)}) copy-start(f32[2,64,16]{2,0,1:T(2,128)S(1)} %all-to-all-done.2) | copy-start | bytes 24580
  432.4 23.0 %all-to-all-start = ((f32[2,64,1024]{2,0,1:T(2,128)}), f32[2,64,1024]{2,0,1:T(2,128)}, u32[]{:S(2)}, u32[]{:S(2)}) async-start(f32[2,64,1024]{2,0,1:T(2,128)} %copy.180), calls=%async_computation | async-start | bytes 1048576 | tf_op jit(solution)/shard_map/all_to_all | solution.py:135
  451.4 31.3 %copy-start.18 = (f32[2,64,1024]{2,1,0:T(8,128)S(1)}, f32[2,64,1024]{2,1,0:T(8,128)}, u32[]{:S(2)}) copy-start(f32[2,64,1024]{2,1,0:T(8,128)} %copy-done.17) | copy-start | bytes 1572868
  451.5 31.2 %copy-start.8 = (f32[2,63,1024]{2,1,0:T(8,128)S(1)}, f32[2,63,1024]{2,1,0:T(8,128)}, u32[]{:S(2)}) copy-start(f32[2,63,1024]{2,1,0:T(8,128)} %copy-done.7) | copy-start | bytes 1548292
  451.5 31.2 %copy-start.9 = (bf16[2,64,1024]{2,1,0:T(8,128)(2,1)S(1)}, bf16[2,64,1024]{2,1,0:T(8,128)(2,1)}, u32[]{:S(2)}) copy-start(bf16[2,64,1024]{2,1,0:T(8,128)(2,1)} %param.25) | copy-start | bytes 786436
  452.9 29.8 %copy-start.27 = (f32[2,64,128]{2,1,0:T(8,128)S(1)}, f32[2,64,128]{2,1,0:T(8,128)}, u32[]{:S(2)}) copy-start(f32[2,64,128]{2,1,0:T(8,128)} %all-reduce.18.cloned.1.call-done) | copy-start | bytes 196612
  452.9 30.8 %copy-start.21 = (f32[2,64,1024]{2,1,0:T(8,128)S(1)}, f32[2,64,1024]{2,1,0:T(8,128)}, u32[]{:S(2)}) copy-start(f32[2,64,1024]{2,1,0:T(8,128)} %get-tuple-element.909) | copy-start | bytes 1572868
  455.4 19.0 %all-to-all-start.3 = ((f32[1,64,16]{2,0,1:T(1,128)}), f32[1,64,16]{2,0,1:T(1,128)S(1)}, u32[]{:S(2)}, u32[]{:S(2)}) async-start(f32[1,64,16]{2,0,1:T(1,128)} %bitcast.87), calls=%async_computation.3 | async-start | bytes 65536 | tf_op jit(solution)/shard_map/all_to_all | solution.py:136
  474.5 8.2 %copy-start.28 = (f32[1,64,16]{2,0,1:T(1,128)}, f32[1,64,16]{2,0,1:T(1,128)S(1)}, u32[]{:S(2)}) copy-start(f32[1,64,16]{2,0,1:T(1,128)S(1)} %all-to-all-done.3) | copy-start | bytes 12292
  474.5 18.7 %all-to-all-start.1 = ((f32[1,64,1024]{2,0,1:T(1,128)}), f32[1,64,1024]{2,0,1:T(1,128)}, u32[]{:S(2)}, u32[]{:S(2)}) async-start(f32[1,64,1024]{2,0,1:T(1,128)} %copy.182), calls=%async_computation.1 | async-start | bytes 524288 | tf_op jit(solution)/shard_map/all_to_all | solution.py:135
  480.0 319.9 %all-reduce.20.cloned.1.call-start = ((), (), s32[]{:S(2)}) async-start(), calls=%async_computation.7 | async-start | bytes 2097152 | tf_op jit(solution)/shard_map/psum | solution.py:261
  497.4 36.2 %copy-start.13 = (f32[64,1024]{1,0:T(8,128)S(1)}, f32[64,1024]{1,0:T(8,128)}, u32[]{:S(2)}) copy-start(f32[64,1024]{1,0:T(8,128)} %get-tuple-element.905) | copy-start | bytes 786436
  530.5 17.3 %copy-start.20 = (f32[128,1024]{1,0:T(8,128)S(1)}, f32[128,1024]{1,0:T(8,128)}, u32[]{:S(2)}) copy-start(f32[128,1024]{1,0:T(8,128)} %convolution_bitcast_fusion.6) | copy-start | bytes 1572868
  530.5 18.7 %copy-start.16 = (f32[63,1024]{1,0:T(8,128)S(1)}, f32[63,1024]{1,0:T(8,128)}, u32[]{:S(2)}) copy-start(f32[63,1024]{1,0:T(8,128)} %copy-done.15) | copy-start | bytes 774148
  530.5 18.7 %copy-start.19 = (bf16[1,64,1024]{2,1,0:T(8,128)(2,1)S(1)}, bf16[1,64,1024]{2,1,0:T(8,128)(2,1)}, u32[]{:S(2)}) copy-start(bf16[1,64,1024]{2,1,0:T(8,128)(2,1)} %param.23) | copy-start | bytes 393220
  547.7 3.3 copy-start.23
Sparse Core Ops, SparseCore 0:
  63.1 41.2 all-reduce.15
  365.2 40.5 all-reduce.17
Sparse Core Ops, SparseCore 1:
  92.1 99.2 all-gather.3
  551.1 181.9 all-reduce.19
where the time goes:
time: 824 us; the launch traced here: 811 us
  blocking collectives  319 us (39%)
  waiting for transfers between devices  145 us (18%)
  local copies, waits for them, and re-layouts  114 us (14%)
  matrix products  97.1 us (12%)
  other arithmetic  85 us (10%)
  starting transfers between devices  33.6 us (4%)
  between operations  16.5 us (2%)
    psum x1, blocking collectives, per_device(): lax.psum((down_grad + down_grad_prompt, up_gradient + up_grad_prompt, dec...  245 us
    all_gather x1, waiting for transfers between devices, per_device(): lax.all_gather(flat_state, 'dp', axis=0, tiled=True)  82.1 us
    all_gather x1, blocking collectives, per_device(): lax.all_gather(last_row, 'dp', axis=0, tiled=True)  48.6 us
    psum x2, waiting for transfers between devices, decay_factor_total(): return lax.psum(partial_row_block, 'mp')  42.2 us
    psum x2, blocking collectives, decay_factor_total(): return lax.psum(partial_row_block, 'mp')  25.7 us
    dot_general x12, other arithmetic, segment_summands(): jnp.einsum('thc,shc,tshc->hts', acceptor_entries, address_entries, decay,...  25.1 us
    all_to_all x2, starting transfers between devices, return_pieces(): lax.all_to_all(parts[1], 'dp', split_axis=1, concat_axis=1, tiled=True)  22.4 us
    dot_general x12, matrix products, segment_summands(): jnp.einsum('shc,shd->hcd', address_entries * jnp.exp(block_end[None] - cu...  21.3 us
  transfers between devices with their start and end apart: 8, of which 7 were waited for; matrix products, arithmetic and copies ran while one was open for 8% of the time, Pallas kernels for 0%

commit v1 on v0

v1 whole, which is shorter than its diff:
```python
import functools

import jax
import jax.numpy as jnp
import numpy as np
from jax import lax
from jax.experimental import pallas as pl
from jax.experimental.pallas import tpu as pltpu
from jax.sharding import PartitionSpec as P

HEAD = 64
T = 64
LANES = 128
RANK = 128
LEVELS = (32, 16, 8, 4, 2, 1)
MESH = pl.DeviceIdType.MESH
F32 = jnp.float32
BF16 = jnp.bfloat16


def stages_of(devices):
    if devices == 64:
        return ((1, 2), (2, 4), (8, 8))
    return ((1, 2), (2, 2), (4, devices // 4))


def gap_masks():
    t = np.arange(T)[:, None]
    j = np.arange(T)[None, :]
    rows = []
    for b in LEVELS:
        same = (t // (2 * b)) == (j // (2 * b))
        mid = (t // (2 * b)) * 2 * b + b
        second = (t % (2 * b)) >= b
        rows.append(same & np.where(second, (j >= mid) & (j < t), (j > t) & (j < mid)))
    rows.append(j < t)
    return np.concatenate(rows, axis=0).astype(np.float32)


def level_masks():
    t = np.arange(T)[:, None]
    s = (np.arange(2 * T) % T)[None, :]
    rows = []
    for b in LEVELS:
        same = (t // (2 * b)) == (s // (2 * b))
        rows.append(same & ((t % (2 * b) >= b) != (s % (2 * b) >= b)))
    return np.concatenate(rows, axis=0).astype(np.float32)


def nn(a, b):
    return lax.dot_general(a, b, (((1,), (0,)), ((), ())), preferred_element_type=F32)


def nt(a, b):
    return lax.dot_general(a, b, (((1,), (1,)), ((), ())), preferred_element_type=F32)


def tn(a, b):
    return lax.dot_general(a, b, (((0,), (0,)), ((), ())), preferred_element_type=F32)


def split(x):
    hi = x.astype(BF16)
    return hi, (x - hi.astype(F32)).astype(BF16)


def split3(x):
    hi = x.astype(BF16)
    rest = x - hi.astype(F32)
    mid = rest.astype(BF16)
    return hi, mid, (rest - mid.astype(F32)).astype(BF16)


def dot3(dot, a, b):
    return dot(a[0], b[0]) + (dot(a[0], b[1]) + dot(a[1], b[0]))


def left2(dot, a, b):
    return dot(a[0], b) + dot(a[1], b)


def right2(dot, a, b):
    return dot(a, b[0]) + dot(a, b[1])


def lane_head(shape):
    return lax.broadcasted_iota(jnp.int32, shape, len(shape) - 1) < HEAD


def block_diag(x):
    low = lane_head(x.shape)
    zero = jnp.zeros_like(x)
    return jnp.concatenate([jnp.where(low, x, zero), jnp.where(low, zero, x)], axis=0)


def pack_diag(m):
    return jnp.where(lane_head((HEAD, LANES)), m[:HEAD], m[HEAD:])


def body(
    devices,
    ranks,
    channels,
    owner_ref,
    child_ref,
    kv_ref,
    xp_ref,
    rkv_ref,
    xr_ref,
    dy_ref,
    down_ref,
    up_ref,
    base_ref,
    u_ref,
    f_ref,
    gaps_ref,
    gaps_t_ref,
    masks_ref,
    rkv_out,
    xr_out,
    kv_out,
    xp_out,
    down_out,
    up_out,
    vec_out,
    row_src,
    row_land,
    mixed,
    hid,
    hid_land,
    lead,
    lead_land,
    dec,
    ef,
    send1,
    recv1,
    send2,
    recv2,
    dr_loc,
    dd_loc,
    th_ref,
    dz_ref,
    dth,
    dth_land,
    dh_src,
    dh_land,
    vec,
    vec_land,
    grad,
    cur1,
    cur2,
    cur3,
    land0,
    land1,
    land2,
    fin,
    row_s,
    row_r,
    hid_s,
    hid_r,
    lead_s,
    lead_r,
    r1_s,
    r1_r,
    r2_s,
    r2_r,
    dth_s,
    dth_r,
    dh_s,
    dh_r,
    vec_s,
    vec_r,
    rs_s,
    rs_r,
    ag_s,
    ag_r,
):
    me = lax.axis_index("dp")
    rank = lax.axis_index("mp")
    pairs = channels // LANES
    per = HEAD * pairs // devices
    dests = HEAD // per
    stages = stages_of(devices)

    def lanes(p):
        return pl.ds(pl.multiple_of(p * LANES, LANES), LANES)

    def rows_of(p):
        return pl.ds(pl.multiple_of(p * LANES, LANES), LANES)

    def loop(n, fn, init=None):
        if init is None:
            lax.fori_loop(0, n, lambda i, c: (fn(i), c)[1], 0)
            return None
        return lax.fori_loop(0, n, fn, init)

    def remote(src, dst, ssem, rsem, axis, peer):
        return pltpu.make_async_remote_copy(
            src_ref=src,
            dst_ref=dst,
            send_sem=ssem,
            recv_sem=rsem,
            device_id={axis: peer},
            device_id_type=MESH,
        )

    def bulk_wait(view, sem):
        pltpu.make_async_copy(view, view, sem).wait()

    barrier = pltpu.get_barrier_semaphore()

    def greet(i):
        pl.semaphore_signal(
            barrier, inc=1, device_id={"dp": lax.rem(me + 1 + i, devices)}, device_id_type=MESH
        )

    loop(devices - 1, greet)
    for i in range(1, ranks):
        pl.semaphore_signal(
            barrier, inc=1, device_id={"mp": lax.rem(rank + i, ranks)}, device_id_type=MESH
        )

    row_src[...] = xp_ref[0, T - 16 :, :].astype(F32)[15:16]
    pl.semaphore_wait(barrier, devices - 1 + ranks - 1)

    def send_row(i):
        peer = lax.rem(me + 1 + i, devices)
        remote(row_src, row_land.at[me], row_s, row_r, "dp", peer).start()

    loop(devices - 1, send_row)
    row_land[me] = row_src[...]

    first_row = lax.broadcasted_iota(jnp.int32, (T, LANES), 0) == 0
    last_row = lax.broadcasted_iota(jnp.int32, (T, LANES), 0) == T - 1

    def x_of(i, p):
        return (xp_ref[0, :, lanes(p)] if i == 0 else xr_ref[i - 1, :, lanes(p)]).astype(F32)

    def mix(p, acc):
        f = f_ref[:, lanes(p)]
        parts = []
        for i in range(3):
            x = x_of(i, p)
            prev = jnp.where(first_row, 0.0, pltpu.roll(x, 1, 0))
            m = x + (prev - x) * f
            mixed[i * T : (i + 1) * T, lanes(p)] = m
            parts.append(m)
        return acc + dot3(nn, split(jnp.concatenate(parts, axis=0)), split(down_ref[rows_of(p), :]))

    hid[...] = loop(pairs, mix, jnp.zeros((3 * T, RANK), F32))

    def exchange(src, land, ssem, rsem):
        for i in range(1, ranks):
            peer = lax.rem(rank + i, ranks)
            remote(src, land.at[rank], ssem.at[i], rsem.at[rank], "mp", peer).start()
        land[rank] = src[...]

    def exchanged(land, rsem):
        for i in range(1, ranks):
            source = lax.rem(rank + i, ranks)
            bulk_wait(land.at[source], rsem.at[source])
        total = land[0]
        for i in range(1, ranks):
            total = total + land[i]
        return total

    exchange(hid, hid_land, hid_s, hid_r)

    bulk_wait(row_land.at[pl.ds(0, devices - 1)], row_r)
    owners = [owner_ref[2 * me + i] for i in range(2)]
    lead_rows = [row_land[o] for o in owners]
    row8 = lax.broadcasted_iota(jnp.int32, (8, channels), 0)
    both = jnp.where(row8 == 0, lead_rows[0], jnp.where(row8 == 1, lead_rows[1], 0.0))
    lead[:, :] = both

    def lead_mix(p, acc):
        fl = f_ref[:, lanes(p)] * lead[:, lanes(p)]
        for i in range(2):
            at = (i + 1) * T
            mixed[at : at + 1, lanes(p)] = mixed[at : at + 1, lanes(p)] + fl[i : i + 1]
        return acc + dot3(nn, split(fl), split(down_ref[rows_of(p), :]))

    lead_hid = loop(pairs, lead_mix, jnp.zeros((8, RANK), F32))
    dh_src[...] = lead_hid
    exchange(dh_src, lead_land, lead_s, lead_r)
    hidden = exchanged(hid_land, hid_r)
    extra = exchanged(lead_land, lead_r)
    th_ref[...] = jnp.tanh(hidden)
    for i in range(2):
        at = (i + 1) * T
        th_ref[at : at + 1, :] = jnp.tanh(hidden[at : at + 1] + extra[i : i + 1])

    before = gaps_ref[len(LEVELS) * T :, :]
    suffix = (
        lax.broadcasted_iota(jnp.int32, (T, T), 1) > lax.broadcasted_iota(jnp.int32, (T, T), 0)
    ).astype(BF16)

    def exact(mask, x):
        hi, mid, low = split3(x)
        return nn(mask, hi) + (nn(mask, mid) + nn(mask, low))

    def decays(p):
        th = split(th_ref[...])
        z = dot3(nn, th, split(up_ref[:, lanes(p)])) + base_ref[:, lanes(p)]
        d = -jnp.exp(z)
        dec[:, lanes(p)] = d
        for i in range(3):
            e = jnp.exp(exact(suffix if i == 0 else before, d[i * T : (i + 1) * T]))
            ef[i * T : (i + 1) * T, lanes(p)] = e
            if i == 0:
                a, b = kv_ref[0, 0, :, lanes(p)], kv_ref[1, 0, :, lanes(p)]
            else:
                a, b = rkv_ref[0, i - 1, :, lanes(p)], dy_ref[i - 1, :, lanes(p)]
            packed = pack_diag(left2(tn, split(a.astype(F32) * e), b))
            send1[pl.ds(p * dests, dests), i] = packed.reshape(dests, per, LANES)

    loop(pairs, decays)

    def route1(i):
        peer = lax.rem(me + 1 + i, devices)
        remote(send1.at[peer], recv1.at[pl.ds(3 * me, 3)], r1_s, r1_r, "dp", peer).start()

    loop(devices - 1, route1)
    recv1[pl.ds(3 * me, 3)] = send1[me]

    ones_block = (
        (lax.broadcasted_iota(jnp.int32, (LANES, LANES), 0) < HEAD)
        == (lax.broadcasted_iota(jnp.int32, (LANES, LANES), 1) < HEAD)
    ).astype(BF16)
    t_row = lax.broadcasted_iota(jnp.int32, (T, LANES), 0)
    s_col = lax.rem(lax.broadcasted_iota(jnp.int32, (T, LANES), 1), T)

    def inner(i, p):
        rb, kb, vb = (rkv_ref[n, i, :, lanes(p)] for n in range(3))
        yb = dy_ref[i, :, lanes(p)]
        r, k, v, y = (a.astype(F32) for a in (rb, kb, vb, yb))
        d = dec[pl.ds((i + 1) * T, T), lanes(p)]
        u = u_ref[:, lanes(p)]
        y_diag = block_diag(yb)
        sym = jnp.where(t_row > s_col, nt(yb, block_diag(vb)), nt(vb, y_diag))
        gap = exact(gaps_ref[: len(LEVELS) * T, :], d)
        att = jnp.zeros((T, LANES), F32)
        dr = jnp.zeros((T, LANES), F32)
        dk = jnp.zeros((T, LANES), F32)
        dgaps = []
        for level, b in enumerate(LEVELS):
            second = lax.rem(t_row, 2 * b) >= b
            mask = masks_ref[level * T : (level + 1) * T, :]
            x = jnp.exp(gap[level * T : (level + 1) * T])
            w = jnp.where(second, r, k) * x
            ws = split(w)
            wd = tuple(block_diag(a) for a in ws)
            att = att + mask * dot3(nt, ws, wd)
            dw = dot3(nn, split(mask * sym), wd)
            dgaps.append(w * dw)
            g = x * dw
            dr = dr + jnp.where(second, g, 0.0)
            dk = dk + jnp.where(second, 0.0, g)
        dgap = jnp.concatenate(dgaps, axis=0)
        dd_loc[i, :, lanes(p)] = right2(nn, gaps_t_ref[:, : len(LEVELS) * T], split(dgap))
        self_a = left2(nn, split(r * u * k), ones_block)
        self_b = left2(nn, split(y * v), ones_block)
        dv = left2(nn, split(jnp.where(s_col > t_row, att, 0.0)), y_diag) + self_a * y
        dr_loc[i, :, lanes(p)] = dr + u * k * self_b
        rkv_out[1, i, :, lanes(p)] = (dk + u * r * self_b).astype(BF16)
        rkv_out[2, i, :, lanes(p)] = dv.astype(BF16)
        part = jnp.sum(r * k * self_b, axis=0, keepdims=True)
        if i == 0:
            vec[1, :, lanes(p)] = part
        else:
            vec[1, :, lanes(p)] = vec[1, :, lanes(p)] + part

    loop(pairs, functools.partial(inner, 0))

    bulk_wait(recv1.at[pl.ds(0, 3 * (devices - 1))], r1_r)

    def shuffle(n):
        send2[n, 0] = recv1[owner_ref[2 * n] * 3]
        send2[n, 1] = recv1[owner_ref[2 * n + 1] * 3]
        send2[n, 2] = recv1[child_ref[2 * n]] + recv1[child_ref[2 * n + 1]]

    loop(devices, shuffle)

    def route2(i):
        peer = lax.rem(me + 1 + i, devices)
        remote(send2.at[peer], recv2.at[me], r2_s, r2_r, "dp", peer).start()

    loop(devices - 1, route2)
    recv2[me] = send2[me]
    loop(pairs, functools.partial(inner, 1))
    bulk_wait(recv2.at[pl.ds(0, devices - 1)], r2_r)

    def outer(p):
        for i in range(3):
            state = recv2[pl.ds(p * dests, dests), (i + 2) % 3].reshape(HEAD, LANES)
            sd = tuple(block_diag(a) for a in split(state))
            e = ef[i * T : (i + 1) * T, lanes(p)]
            if i == 0:
                kb, vb = kv_ref[0, 0, :, lanes(p)], kv_ref[1, 0, :, lanes(p)]
                k = kb.astype(F32)
                dk = e * right2(nt, vb, sd)
                dv = dot3(nn, split(k * e), sd)
                kv_out[0, 0, :, lanes(p)] = dk.astype(BF16)
                kv_out[1, 0, :, lanes(p)] = dv.astype(BF16)
                dd = right2(nn, before, split(k * dk))
            else:
                r = rkv_ref[0, i - 1, :, lanes(p)].astype(F32)
                drs = e * right2(nt, dy_ref[i - 1, :, lanes(p)], sd)
                rkv_out[0, i - 1, :, lanes(p)] = (dr_loc[i - 1, :, lanes(p)] + drs).astype(BF16)
                dd = right2(nn, suffix, split(r * drs)) + dd_loc[i - 1, :, lanes(p)]
            dz_ref[i * T : (i + 1) * T, lanes(p)] = dd * dec[i * T : (i + 1) * T, lanes(p)]

    loop(pairs, outer)

    def dth_part(p, acc):
        return acc + dot3(nt, split(dz_ref[:, lanes(p)]), split(up_ref[:, lanes(p)]))

    dth[...] = loop(pairs, dth_part, jnp.zeros((3 * T, RANK), F32))
    exchange(dth, dth_land, dth_s, dth_r)

    place = [lax.rem(me // g, n) for g, n in stages]
    size = [channels]
    for g, n in stages:
        size.append(size[-1] // n)
    lands = (land0, land1, land2)
    sums = (cur1, cur2, cur3)

    def rs_start(half, stage):
        g, n = stages[stage]
        q, rows = place[stage], size[stage + 1]
        src = grad.at[half] if stage == 0 else sums[stage - 1].at[half]
        for i in range(1, n):
            other = lax.rem(q + i, n)
            remote(
                src.at[pl.ds(pl.multiple_of(other * rows, 8), rows)],
                lands[stage].at[half, q],
                rs_s.at[half, stage, i],
                rs_r.at[half, stage, q],
                "dp",
                me + (other - q) * g,
            ).start()

    def rs_finish(half, stage):
        g, n = stages[stage]
        q, rows = place[stage], size[stage + 1]
        src = grad.at[half] if stage == 0 else sums[stage - 1].at[half]
        total = src[pl.ds(pl.multiple_of(q * rows, 8), rows), :]
        for i in range(1, n):
            other = lax.rem(q + i, n)
            bulk_wait(lands[stage].at[half, other], rs_r.at[half, stage, other])
            total = total + lands[stage][half, other]
        sums[stage][half] = total

    offs = [0]
    for stage in range(3):
        offs.append(offs[-1] + place[stage] * size[stage + 1])

    def piece(half, stage, q):
        rows = size[stage + 1]
        return fin.at[half, pl.ds(pl.multiple_of(offs[stage] + q * rows, 8), rows)]

    def ag_start(half, stage):
        g, n = stages[stage]
        q = place[stage]
        if stage == 2:
            fin[half, pl.ds(pl.multiple_of(offs[3], 8), size[3]), :] = sums[2][half]
        for i in range(1, n):
            other = lax.rem(q + i, n)
            mine = piece(half, stage, q)
            remote(
                mine,
                mine,
                ag_s.at[half, stage, i],
                ag_r.at[half, stage, q],
                "dp",
                me + (other - q) * g,
            ).start()

    def ag_finish(half, stage):
        g, n = stages[stage]
        q = place[stage]
        for i in range(1, n):
            other = lax.rem(q + i, n)
            bulk_wait(piece(half, stage, other), ag_r.at[half, stage, other])

    def vec_start(stage):
        g, n = stages[stage]
        q = place[stage]
        at = sum(m for _, m in stages[:stage])
        for i in range(1, n):
            other = lax.rem(q + i, n)
            remote(
                vec.at[pl.ds(3 * stage, 3)],
                vec_land.at[at + q],
                vec_s.at[stage, i],
                vec_r.at[stage, q],
                "dp",
                me + (other - q) * g,
            ).start()
        vec_land[at + q] = vec[3 * stage : 3 * stage + 3]

    def vec_finish(stage):
        g, n = stages[stage]
        q = place[stage]
        at = sum(m for _, m in stages[:stage])
        for i in range(1, n):
            other = lax.rem(q + i, n)
            bulk_wait(vec_land.at[at + other], vec_r.at[stage, other])
        total = vec_land[at]
        for i in range(1, n):
            total = total + vec_land[at + i]
        if stage == 2:
            vec_out[...] = total
        else:
            vec[3 * stage + 3 : 3 * stage + 6] = total

    def up_grads(p):
        dz = dz_ref[:, lanes(p)]
        grad[0, rows_of(p), :] = dot3(tn, split(th_ref[...]), split(dz))
        vec[0, :, lanes(p)] = jnp.sum(dz, axis=0, keepdims=True)

    loop(pairs, up_grads)
    rs_start(0, 0)

    th = th_ref[...]
    dh = exchanged(dth_land, dth_r) * (1.0 - th * th)
    row8h = lax.broadcasted_iota(jnp.int32, (8, RANK), 0)
    for i in range(1, ranks):
        bulk_wait(lead_land.at[0], lead_s.at[i])
        bulk_wait(dth_land.at[0], dth_s.at[i])
    dth[...] = dh
    dh_src[...] = jnp.where(
        row8h == 0, dh[T : T + 1], jnp.where(row8h == 1, dh[2 * T : 2 * T + 1], 0.0)
    )

    def send_dh(i):
        peer = lax.rem(me + 1 + i, devices)
        remote(dh_src, dh_land.at[me], dh_s, dh_r, "dp", peer).start()

    loop(devices - 1, send_dh)
    dh_land[me] = dh_src[...]

    def down_grads(p):
        grad[1, rows_of(p), :] = dot3(tn, split(mixed[:, lanes(p)]), split(dth[...]))

    loop(pairs, down_grads)
    rs_start(1, 0)

    bulk_wait(dh_land.at[pl.ds(0, devices - 1)], dh_r)
    from_children = jnp.zeros((8, RANK), F32)
    for i in range(2):
        c = child_ref[2 * me + i]
        slot = lax.div(c, 3)
        which = lax.rem(c, 3)
        rows = dh_land[slot]
        from_children = from_children + jnp.sum(
            jnp.where(row8h == which - 1, rows, 0.0), axis=0, keepdims=True
        )

    def x_grads(p):
        f = f_ref[:, lanes(p)]
        n = split(down_ref[rows_of(p), :])
        dm = dot3(nt, split(dth[...]), n)
        late = dot3(nt, split(from_children), n)[0:1]
        mix_sum = jnp.zeros((1, LANES), F32)
        for i in range(3):
            x = x_of(i, p)
            g = dm[i * T : (i + 1) * T]
            ahead = pltpu.roll(g, T - 1, 0)
            if i == 0:
                first = jnp.zeros((1, LANES), F32)
                ahead = jnp.where(last_row, late, ahead)
            else:
                first = lead[i - 1 : i, lanes(p)]
                ahead = jnp.where(last_row, 0.0, ahead)
            prev = jnp.where(first_row, first, pltpu.roll(x, 1, 0))
            dx = g + (ahead - g) * f
            mix_sum = mix_sum + jnp.sum(g * (prev - x), axis=0, keepdims=True)
            if i == 0:
                xp_out[0, :, lanes(p)] = dx.astype(BF16)
            else:
                xr_out[i - 1, :, lanes(p)] = dx.astype(BF16)
        vec[2, :, lanes(p)] = mix_sum

    rs_finish(0, 0)
    rs_start(0, 1)
    loop(pairs, x_grads)
    vec_start(0)
    rs_finish(1, 0)
    rs_start(1, 1)
    rs_finish(0, 1)
    rs_start(0, 2)
    vec_finish(0)
    vec_start(1)
    rs_finish(1, 1)
    rs_start(1, 2)
    rs_finish(0, 2)
    ag_start(0, 2)
    vec_finish(1)
    vec_start(2)
    rs_finish(1, 2)
    ag_start(1, 2)
    ag_finish(0, 2)
    ag_start(0, 1)
    vec_finish(2)
    ag_finish(1, 2)
    ag_start(1, 1)
    ag_finish(0, 1)
    ag_start(0, 0)
    ag_finish(1, 1)
    ag_start(1, 0)
    ag_finish(0, 0)

    def put_up(p):
        up_out[:, lanes(p)] = fin[0, rows_of(p), :]

    loop(pairs, put_up)
    ag_finish(1, 0)
    down_out[...] = fin[1]

    bulk_wait(row_land.at[pl.ds(0, devices - 1)], row_s)
    bulk_wait(recv1.at[pl.ds(0, 3 * (devices - 1))], r1_s)
    bulk_wait(recv2.at[pl.ds(0, devices - 1)], r2_s)
    bulk_wait(dh_land.at[pl.ds(0, devices - 1)], dh_s)
    for i in range(1, ranks):
        bulk_wait(hid_land.at[0], hid_s.at[i])
    for stage, (g, n) in enumerate(stages):
        for i in range(1, n):
            bulk_wait(vec_land.at[0], vec_s.at[stage, i])
            for half in range(2):
                bulk_wait(lands[stage].at[half, 0], rs_s.at[half, stage, i])
                bulk_wait(piece(half, stage, place[stage]), ag_s.at[half, stage, i])


def per_device(
    query_text_memory,
    query_text_feed,
    reply_acceptor_memory,
    reply_feed,
    reply_cotangent_vector,
    query_placement,
    reply_parent_query,
    fading_narrowing,
    fading_widening,
    fading_anchor_rate,
    self_emphasis,
    lagged_token_fraction,
):
    devices = lax.axis_size("dp")
    ranks = lax.axis_size("mp")
    channels = query_text_feed.shape[2]
    pairs = channels // LANES
    per = HEAD * pairs // devices
    responses = reply_parent_query.shape[0]
    matches = query_placement[None, :] == reply_parent_query[:, None]
    slots = jnp.arange(devices, dtype=jnp.int32)
    owner = jnp.sum(jnp.where(matches, slots[None, :], 0), axis=1).astype(jnp.int32)
    index = jnp.arange(responses, dtype=jnp.int32)
    index = (index + index // 2 + 1)[:, None]
    first = jnp.min(jnp.where(matches, index, 3 * responses), axis=0)
    last = jnp.max(jnp.where(matches, index, -1), axis=0)
    child = jnp.stack([first, last], axis=1).reshape(-1).astype(jnp.int32)
    gaps = gap_masks()
    stages = stages_of(devices)
    size = [channels]
    for g, n in stages:
        size.append(size[-1] // n)

    def vmem(*shape, dtype=F32):
        return pltpu.VMEM(shape, dtype)

    dma = pltpu.SemaphoreType.DMA
    scratch = [
        vmem(1, channels),
        vmem(devices, 1, channels),
        vmem(3 * T, channels),
        vmem(3 * T, RANK),
        vmem(ranks, 3 * T, RANK),
        vmem(8, channels),
        vmem(ranks, 8, RANK),
        vmem(3 * T, channels),
        vmem(3 * T, channels),
        vmem(devices, 3, per, LANES),
        vmem(3 * devices, per, LANES),
        vmem(devices, 3, per, LANES),
        vmem(devices, 3, per, LANES),
        vmem(2, T, channels),
        vmem(2, T, channels),
        vmem(3 * T, RANK),
        vmem(3 * T, channels),
        vmem(3 * T, RANK),
        vmem(ranks, 3 * T, RANK),
        vmem(8, RANK),
        vmem(devices, 8, RANK),
        vmem(9, 1, channels),
        vmem(sum(n for _, n in stages), 3, 1, channels),
        vmem(2, channels, RANK),
        vmem(2, size[1], RANK),
        vmem(2, size[2], RANK),
        vmem(2, size[3], RANK),
        vmem(2, stages[0][1], size[1], RANK),
        vmem(2, stages[1][1], size[2], RANK),
        vmem(2, stages[2][1], size[3], RANK),
        vmem(2, channels, RANK),
        dma,
        dma,
        dma((ranks,)),
        dma((ranks,)),
        dma((ranks,)),
        dma((ranks,)),
        dma,
        dma,
        dma,
        dma,
        dma((ranks,)),
        dma((ranks,)),
        dma,
        dma,
        dma((3, 8)),
        dma((3, 8)),
        dma((2, 3, 8)),
        dma((2, 3, 8)),
        dma((2, 3, 8)),
        dma((2, 3, 8)),
    ]
    whole = pl.BlockSpec(memory_space=pltpu.VMEM)
    scalars = pl.BlockSpec(memory_space=pltpu.SMEM)
    rkv, xr, kv, xp, down, up, vec = pl.pallas_call(
        functools.partial(body, devices, ranks, channels),
        out_shape=(
            jax.ShapeDtypeStruct(reply_acceptor_memory.shape, BF16),
            jax.ShapeDtypeStruct(reply_feed.shape, BF16),
            jax.ShapeDtypeStruct(query_text_memory.shape, BF16),
            jax.ShapeDtypeStruct(query_text_feed.shape, BF16),
            jax.ShapeDtypeStruct(fading_narrowing.shape, F32),
            jax.ShapeDtypeStruct(fading_widening.shape, F32),
            jax.ShapeDtypeStruct((3, 1, channels), F32),
        ),
        in_specs=[scalars] * 2 + [whole] * 13,
        out_specs=[whole] * 7,
        scratch_shapes=scratch,
        compiler_params=pltpu.CompilerParams(
            collective_id=0, has_side_effects=True, vmem_limit_bytes=48 * 1024 * 1024
        ),
    )(
        owner,
        child,
        query_text_memory,
        query_text_feed,
        reply_acceptor_memory,
        reply_feed,
        reply_cotangent_vector,
        fading_narrowing,
        fading_widening,
        fading_anchor_rate[None],
        self_emphasis[None],
        lagged_token_fraction[None],
        jnp.asarray(gaps, BF16),
        jnp.asarray(gaps.T, BF16),
        jnp.asarray(level_masks(), F32),
    )
    return rkv, xr, kv, xp, down, up, vec[0, 0], vec[1, 0], vec[2, 0]


def solution(mesh):
    in_specs = (
        P(None, "dp", None, "mp"),
        P("dp", None, "mp"),
        P(None, "dp", None, "mp"),
        P("dp", None, "mp"),
        P("dp", None, "mp"),
        P(),
        P(),
        P("mp", None),
        P(None, "mp"),
        P("mp"),
        P("mp"),
        P("mp"),
    )
    out_specs = (
        P(None, "dp", None, "mp"),
        P("dp", None, "mp"),
        P(None, "dp", None, "mp"),
        P("dp", None, "mp"),
        P("mp", None),
        P(None, "mp"),
        P("mp"),
        P("mp"),
        P("mp"),
    )
    return jax.shard_map(
        per_device, mesh=mesh, in_specs=in_specs, out_specs=out_specs, check_vma=False
    )
```

time: 824 us -> 143 us (0.17); the launches traced: 811 us -> 143 us
  blocking collectives: 319 us -> 0 us
  waiting for transfers between devices: 145 us -> 0 us
  Pallas kernels: 0 us -> 126 us
  local copies, waits for them, and re-layouts: 114 us -> 14.7 us
  matrix products: 97.1 us -> 0 us
  other arithmetic: 85 us -> 0.91 us
  starting transfers between devices: 33.6 us -> 0 us
  between operations: 16.5 us -> 0.72 us
    psum x3 -> x0, blocking collectives: 270 us -> none  [the longest x1 245 us: per_device(): lax.psum((down_grad + down_grad_prompt, up_gradient + up_grad_prompt, dec...]
    pallas_call x0 -> x1, Pallas kernels: none -> 126 us  [per_device(): pl.pallas_call(functools.partial(body, devices, ranks, channels), out_sha...]
    dot_general x56 -> x0, matrix products: 97.1 us -> none  [the longest x12 21.3 us: segment_summands(): jnp.einsum('shc,shd->hcd', address_entries * jnp.exp(block_end[None] - cu...]
    all_gather x1 -> x0, waiting for transfers between devices: 82.1 us -> none  [per_device(): lax.all_gather(flat_state, 'dp', axis=0, tiled=True)]
    all_gather x1 -> x0, blocking collectives: 48.6 us -> none  [per_device(): lax.all_gather(last_row, 'dp', axis=0, tiled=True)]
    psum x3 -> x0, waiting for transfers between devices: 42.2 us -> none  [the longest x2 42.2 us: decay_factor_total(): return lax.psum(partial_row_block, 'mp')]
    all_to_all x4 -> x0, starting transfers between devices: 33.1 us -> none  [the longest x2 22.4 us: return_pieces(): lax.all_to_all(parts[1], 'dp', split_axis=1, concat_axis=1, tiled=True)]
    dot_general x12 -> x0, other arithmetic: 25.1 us -> none  [segment_summands(): jnp.einsum('thc,shc,tshc->hts', acceptor_entries, address_entries, decay,...]
  transfers between devices with their start and end apart: 8 -> 0, of which waited for: 7 -> 0; matrix products, arithmetic and copies ran while one was open for 8% -> 0% of each run, Pallas kernels for 0% -> 0%
where the time goes in v1:
time: 143 us
  Pallas kernels  126 us (88%)
  local copies, waits for them, and re-layouts  14.7 us (10%)
    pallas_call x1, Pallas kernels, per_device(): pl.pallas_call(functools.partial(body, devices, ranks, channels), out_sha...  126 us
    unnamed x32, local copies, waits for them, and re-layouts  13.9 us

profile of v1, /device:TPU:1, one launch (start us, length us, event | category | flops | bytes accessed | tf_op | source)
XLA Modules:
  0.0 142.8 jit_solution(11829340082042802414)
XLA Ops:
  0.6 0.0 copy-start.9
  0.7 0.9 fusion.1
  1.6 0.1 copy.26
  1.7 0.0 copy-start.10
  1.7 0.0 copy-start.11
  1.7 0.0 copy-start.12
  1.7 0.1 reshape.39.child_ref
  1.8 0.0 copy-done.9
  1.9 0.5 copy-done.10
  2.4 0.0 copy-done.11
  2.4 0.0 copy-done.12
  2.4 0.0 copy-start
  2.4 1.1 copy-done
  3.5 0.0 copy-start.1
  3.5 1.0 copy-done.1
  4.6 0.0 copy-start.2
  4.6 1.0 copy-done.2
  5.6 0.0 copy-start.3
  5.6 0.9 copy-done.3
  6.6 0.0 copy-start.4
  6.6 0.9 copy-done.4
  7.5 0.0 copy-start.5
  7.5 0.9 copy-done.5
  8.5 0.0 copy-start.6
  8.5 0.9 copy-done.6
  9.4 0.0 copy-start.7
  9.4 0.9 copy-done.7
  10.3 0.0 copy-start.8
  10.3 0.9 copy-done.8
  11.2 126.4 %shard_map.214 = (bf16[3,2,64,1024]{3,2,1,0:T(8,128)(2,1)S(1)}, bf16[2,64,1024]{2,1,0:T(8,128)(2,1)S(1)}, bf16[2,1,64,1024]{3,2,1,0:T(8,128)(2,1)S(1)}, bf16[1,6...) custom-call(s32[128]{0:T(128)S(1)} %get-tuple-element.25.owner_ref, ...), custom_call_target="tpu_custom_call" | custom-call | tf_op jit(solution)/shard_map/pallas_call | solution.py:728
  137.7 0.6 fusion.4
  138.3 0.9 copy.33
  139.1 0.7 copy.34
  139.8 0.7 copy.35
  140.5 0.7 copy.36
  141.2 0.8 copy.37
  142.0 0.8 copy.38
  (2 shorter events, 0.0 us)
Async XLA Ops:
  0.6 1.2 copy-start.9
  1.7 0.7 copy-start.10
  1.7 0.7 copy-start.11
  1.7 0.7 copy-start.12
  2.4 1.1 copy-start
  3.5 1.0 copy-start.1
  4.6 1.0 copy-start.2
  5.6 0.9 copy-start.3
  6.6 0.9 copy-start.4
  7.5 0.9 copy-start.5
  8.5 0.9 copy-start.6
  9.4 0.9 copy-start.7
  10.3 0.9 copy-start.8

commit v2 on v1

v2 whole, which is shorter than its diff:
```python
import functools

import jax
import jax.numpy as jnp
from jax import lax
from jax.experimental import pallas as pl
from jax.experimental.pallas import tpu as pltpu
from jax.sharding import PartitionSpec as P

HEAD = 64
T = 64
LANES = 128
RANK = 128
VMEM = 63 * 1024 * 1024
LEVELS = (32, 16, 8, 4, 2, 1)
MESH = pl.DeviceIdType.MESH
F32 = jnp.float32
BF16 = jnp.bfloat16


def stages_of(devices):
    if devices == 64:
        return ((1, 2), (2, 4), (8, 8))
    return ((1, 2), (2, 2), (4, devices // 4))


def nn(a, b):
    return lax.dot_general(a, b, (((1,), (0,)), ((), ())), preferred_element_type=F32)


def nt(a, b):
    return lax.dot_general(a, b, (((1,), (1,)), ((), ())), preferred_element_type=F32)


def tn(a, b):
    return lax.dot_general(a, b, (((0,), (0,)), ((), ())), preferred_element_type=F32)


def split(x):
    hi = x.astype(BF16)
    return hi, (x - hi.astype(F32)).astype(BF16)


def split3(x):
    hi = x.astype(BF16)
    rest = x - hi.astype(F32)
    mid = rest.astype(BF16)
    return hi, mid, (rest - mid.astype(F32)).astype(BF16)


def dot3(dot, a, b):
    return dot(a[0], b[0]) + (dot(a[0], b[1]) + dot(a[1], b[0]))


def left2(dot, a, b):
    return dot(a[0], b) + dot(a[1], b)


def right2(dot, a, b):
    return dot(a, b[0]) + dot(a, b[1])


def lane_head(shape):
    return lax.broadcasted_iota(jnp.int32, shape, len(shape) - 1) < HEAD


def block_diag(x):
    low = lane_head(x.shape)
    zero = jnp.zeros_like(x)
    return jnp.concatenate([jnp.where(low, x, zero), jnp.where(low, zero, x)], axis=0)


def pack_diag(m):
    return jnp.where(lane_head((HEAD, LANES)), m[:HEAD], m[HEAD:])


def body(
    devices,
    ranks,
    channels,
    owner_ref,
    first_ref,
    last_ref,
    kv_hbm,
    xp_hbm,
    rkv_hbm,
    xr_hbm,
    dy_hbm,
    down_hbm,
    up_hbm,
    base_hbm,
    u_hbm,
    f_hbm,
    rkv_hbm_out,
    xr_hbm_out,
    kv_hbm_out,
    xp_hbm_out,
    grad_hbm_out,
    vec_hbm_out,
    rkv_out,
    xr_out,
    kv_out,
    xp_out,
    vec_out,
    kv_ref,
    xp_ref,
    rkv_ref,
    xr_ref,
    dy_ref,
    down_ref,
    up_ref,
    base_ref,
    u_ref,
    f_ref,
    gaps_ref,
    gaps_t_ref,
    masks_ref,
    row_src,
    row_land,
    mixed,
    hid_p,
    hid_p_land,
    hid_r,
    hid_r_land,
    lead,
    lead_hid,
    lead_land,
    dec,
    ef,
    send_f1,
    recv_f1,
    send_b1,
    recv_b1,
    send_f2,
    recv_f2,
    send_b2,
    recv_b2,
    dr_loc,
    dd_loc,
    th_ref,
    dz_ref,
    dth_r_src,
    dth_r_land,
    dth_p_src,
    dth_p_land,
    dh_ref,
    dh_land,
    xp_tail,
    vec,
    vec_land,
    grad,
    cur1,
    cur2,
    cur3,
    land0,
    land1,
    land2,
    fin,
    in_sem,
    out_sem,
    row_s,
    row_r,
    hid_p_s,
    hid_p_r,
    hid_r_s,
    hid_r_r,
    lead_s,
    lead_r,
    route_s,
    route_r,
    dth_r_s,
    dth_r_r,
    dth_p_s,
    dth_p_r,
    dh_s,
    dh_r,
    vec_s,
    vec_r,
    rs_s,
    rs_r,
    ag_s,
    ag_r,
):
    me = lax.axis_index("dp")
    rank = lax.axis_index("mp")
    pairs = channels // LANES
    per = HEAD * pairs // devices
    dests = HEAD // per
    stages = stages_of(devices)

    def lanes(p):
        return pl.ds(pl.multiple_of(p * LANES, LANES), LANES)

    rows_of = lanes

    def loop(n, fn, init=None):
        if init is None:
            lax.fori_loop(0, n, lambda i, c: (fn(i), c)[1], 0)
            return None
        return lax.fori_loop(0, n, fn, init)

    def remote(src, dst, ssem, rsem, axis, peer):
        return pltpu.make_async_remote_copy(
            src_ref=src,
            dst_ref=dst,
            send_sem=ssem,
            recv_sem=rsem,
            device_id={axis: peer},
            device_id_type=MESH,
        )

    def bulk_wait(view, sem):
        pltpu.make_async_copy(view, view, sem).wait()

    barrier = pltpu.get_barrier_semaphore()

    def greet(i):
        pl.semaphore_signal(
            barrier, inc=1, device_id={"dp": lax.rem(me + 1 + i, devices)}, device_id_type=MESH
        )

    for i in range(1, ranks):
        pl.semaphore_signal(
            barrier, inc=1, device_id={"mp": lax.rem(rank + i, ranks)}, device_id_type=MESH
        )
    loop(devices - 1, greet)

    fetches = [
        pltpu.make_async_copy(src, dst, in_sem.at[n])
        for n, (src, dst) in enumerate(
            (
                (xp_hbm, xp_ref),
                (xr_hbm, xr_ref),
                (f_hbm, f_ref),
                (down_hbm, down_ref),
                (up_hbm, up_ref),
                (base_hbm, base_ref),
                (kv_hbm, kv_ref),
                (rkv_hbm, rkv_ref),
                (dy_hbm, dy_ref),
                (u_hbm, u_ref),
            )
        )
    ]
    for fetch in fetches:
        fetch.start()

    stores = []

    def store(src, dst):
        copy = pltpu.make_async_copy(src, dst, out_sem.at[len(stores)])
        copy.start()
        stores.append(copy)

    def gap_mask(shape, t_axis, level):
        t = lax.broadcasted_iota(jnp.int32, shape, t_axis)
        j = lax.broadcasted_iota(jnp.int32, shape, 1 - t_axis)
        if level == len(LEVELS):
            return (j < t).astype(F32).astype(BF16)
        b = LEVELS[level]
        second = (t & b) != 0
        late = second & (j >= (t & -b)) & (j < t)
        early = ~second & (j > t) & (j <= (t | (b - 1)))
        return (late | early).astype(F32).astype(BF16)

    for level in range(len(LEVELS) + 1):
        gaps_ref[level * T : (level + 1) * T, :] = gap_mask((T, T), 0, level)
    for level in range(0, len(LEVELS), 2):
        both = [gap_mask((T, T), 1, level + n) for n in range(2)]
        gaps_t_ref[:, level * T : (level + 2) * T] = jnp.concatenate(both, axis=1)
    t_row = lax.broadcasted_iota(jnp.int32, (T, LANES), 0)
    s_col = lax.broadcasted_iota(jnp.int32, (T, LANES), 1) & (T - 1)
    apart = t_row ^ s_col
    for level, b in enumerate(LEVELS):
        masks_ref[level * T : (level + 1) * T, :] = ((apart >= b) & (apart < 2 * b)).astype(F32)

    first_row = lax.broadcasted_iota(jnp.int32, (T, LANES), 0) == 0
    last_row = lax.broadcasted_iota(jnp.int32, (T, LANES), 0) == T - 1

    def x_of(i, p):
        return (xp_ref[0, :, lanes(p)] if i == 0 else xr_ref[i - 1, :, lanes(p)]).astype(F32)

    def mix(p, acc):
        f = f_ref[:, lanes(p)]
        parts = []
        for i in range(3):
            x = x_of(i, p)
            prev = jnp.where(first_row, 0.0, pltpu.roll(x, 1, 0))
            m = x + (prev - x) * f
            mixed[i * T : (i + 1) * T, lanes(p)] = m
            parts.append(m)
        return acc + dot3(nn, split(jnp.concatenate(parts, axis=0)), split(down_ref[rows_of(p), :]))

    for fetch in fetches[:4]:
        fetch.wait()
    row_src[...] = xp_ref[0, T - 16 :, :].astype(F32)[15:16]
    partial = loop(pairs, mix, jnp.zeros((3 * T, RANK), F32))
    hid_p[...] = partial[:T]
    hid_r[...] = partial[T:]
    for fetch in fetches[4:]:
        fetch.wait()
    pl.semaphore_wait(barrier, devices - 1 + ranks - 1)

    def exchange(src, land, ssem, rsem):
        for i in range(1, ranks):
            peer = lax.rem(rank + i, ranks)
            remote(src, land.at[rank], ssem.at[i], rsem.at[rank], "mp", peer).start()
        land[rank] = src[...]

    def exchanged(land, rsem):
        for i in range(1, ranks):
            source = lax.rem(rank + i, ranks)
            bulk_wait(land.at[source], rsem.at[source])
        total = land[0]
        for i in range(1, ranks):
            total = total + land[i]
        return total

    def send_row(i):
        peer = lax.rem(me + 1 + i, devices)
        remote(row_src, row_land.at[me], row_s, row_r, "dp", peer).start()

    exchange(hid_p, hid_p_land, hid_p_s, hid_p_r)
    loop(devices - 1, send_row)
    row_land[me] = row_src[...]
    exchange(hid_r, hid_r_land, hid_r_s, hid_r_r)
    before = gaps_ref[len(LEVELS) * T :, :]
    suffix = (
        lax.broadcasted_iota(jnp.int32, (T, T), 1) > lax.broadcasted_iota(jnp.int32, (T, T), 0)
    ).astype(F32).astype(BF16)

    def exact(mask, x):
        hi, mid, low = split3(x)
        return nn(mask, hi) + (nn(mask, mid) + nn(mask, low))

    def decays(lo, hi, p):
        z = dot3(nn, split(th_ref[lo * T : hi * T, :]), split(up_ref[:, lanes(p)]))
        d = -jnp.exp(z + base_ref[:, lanes(p)])
        dec[lo * T : hi * T, lanes(p)] = d
        for i in range(lo, hi):
            at = (i - lo) * T
            e = jnp.exp(exact(suffix if i == 0 else before, d[at : at + T]))
            ef[i * T : (i + 1) * T, lanes(p)] = e
            if i == 0:
                a, b = kv_ref[0, 0, :, lanes(p)], kv_ref[1, 0, :, lanes(p)]
            else:
                a, b = rkv_ref[0, i - 1, :, lanes(p)], dy_ref[i - 1, :, lanes(p)]
            packed = pack_diag(left2(tn, split(a.astype(F32) * e), b)).reshape(dests, per, LANES)
            if i == 0:
                send_f1[pl.ds(p * dests, dests)] = packed
            else:
                send_b1[pl.ds(p * dests, dests), i - 1] = packed

    def route(n, src, dst_of):
        def send(i):
            peer = lax.rem(me + 1 + i, devices)
            remote(src.at[peer], dst_of(me), route_s.at[n], route_r.at[n], "dp", peer).start()

        loop(devices - 1, send)

    th_ref[:T, :] = jnp.tanh(exchanged(hid_p_land, hid_p_r))
    loop(pairs, functools.partial(decays, 0, 1))
    route(0, send_f1, lambda m: recv_f1.at[m])
    recv_f1[me] = send_f1[me]

    bulk_wait(row_land.at[pl.ds(0, devices - 1)], row_r)
    lead_rows = [row_land[owner_ref[2 * me + i]] for i in range(2)]
    row8 = lax.broadcasted_iota(jnp.int32, (8, channels), 0)
    lead[...] = jnp.where(row8 == 0, lead_rows[0], jnp.where(row8 == 1, lead_rows[1], 0.0))

    def lead_mix(p, acc):
        fl = f_ref[:, lanes(p)] * lead[:, lanes(p)]
        for i in range(2):
            at = (i + 1) * T
            mixed[at : at + 1, lanes(p)] = mixed[at : at + 1, lanes(p)] + fl[i : i + 1]
        return acc + dot3(nn, split(fl), split(down_ref[rows_of(p), :]))

    lead_hid[...] = loop(pairs, lead_mix, jnp.zeros((8, RANK), F32))
    exchange(lead_hid, lead_land, lead_s, lead_r)
    hidden = exchanged(hid_r_land, hid_r_r)
    th_ref[T:, :] = jnp.tanh(hidden)
    extra = exchanged(lead_land, lead_r)
    for i in range(2):
        at = (i + 1) * T
        th_ref[at : at + 1, :] = jnp.tanh(hidden[i * T : i * T + 1] + extra[i : i + 1])
    loop(pairs, functools.partial(decays, 1, 3))
    route(1, send_b1, lambda m: recv_b1.at[pl.ds(2 * m, 2)])
    recv_b1[pl.ds(2 * me, 2)] = send_b1[me]

    bulk_wait(recv_f1.at[pl.ds(0, devices - 1)], route_r.at[0])

    def shuffle_f(n):
        send_f2[n, 0] = recv_f1[owner_ref[2 * n]]
        send_f2[n, 1] = recv_f1[owner_ref[2 * n + 1]]

    loop(devices, shuffle_f)
    route(2, send_f2, lambda m: recv_f2.at[m])
    recv_f2[me] = send_f2[me]

    ones_block = (
        (
            (lax.broadcasted_iota(jnp.int32, (LANES, LANES), 0) < HEAD)
            == (lax.broadcasted_iota(jnp.int32, (LANES, LANES), 1) < HEAD)
        )
        .astype(F32)
        .astype(BF16)
    )

    def inner(i, p):
        rb, kb, vb = (rkv_ref[n, i, :, lanes(p)] for n in range(3))
        yb = dy_ref[i, :, lanes(p)]
        r, k, v, y = (a.astype(F32) for a in (rb, kb, vb, yb))
        d = dec[(i + 1) * T : (i + 2) * T, lanes(p)]
        u = u_ref[:, lanes(p)]
        y_diag = block_diag(yb)
        sym = jnp.where(t_row > s_col, nt(yb, block_diag(vb)), nt(vb, y_diag))
        gap = exact(gaps_ref[: len(LEVELS) * T, :], d)
        att = jnp.zeros((T, LANES), F32)
        dr = jnp.zeros((T, LANES), F32)
        dk = jnp.zeros((T, LANES), F32)
        dgaps = []
        for level, b in enumerate(LEVELS):
            second = (t_row & b) != 0
            mask = masks_ref[level * T : (level + 1) * T, :]
            x = jnp.exp(gap[level * T : (level + 1) * T])
            w = jnp.where(second, r, k) * x
            ws = split(w)
            wd = tuple(block_diag(a) for a in ws)
            att = att + mask * dot3(nt, ws, wd)
            dw = dot3(nn, split(mask * sym), wd)
            dgaps.append(w * dw)
            g = x * dw
            dr = dr + jnp.where(second, g, 0.0)
            dk = dk + jnp.where(second, 0.0, g)
        dgap = jnp.concatenate(dgaps, axis=0)
        dd_loc[i, :, lanes(p)] = right2(nn, gaps_t_ref[...], split(dgap))
        self_a = left2(nn, split(r * u * k), ones_block)
        self_b = left2(nn, split(y * v), ones_block)
        dv = left2(nn, split(jnp.where(s_col > t_row, att, 0.0)), y_diag) + self_a * y
        dr_loc[i, :, lanes(p)] = dr + u * k * self_b
        rkv_out[1, i, :, lanes(p)] = (dk + u * r * self_b).astype(BF16)
        rkv_out[2, i, :, lanes(p)] = dv.astype(BF16)
        part = jnp.sum(r * k * self_b, axis=0, keepdims=True)
        if i == 0:
            vec[1, :, lanes(p)] = part
        else:
            vec[1, :, lanes(p)] = vec[1, :, lanes(p)] + part

    loop(pairs, functools.partial(inner, 0))
    bulk_wait(recv_b1.at[pl.ds(0, 2 * (devices - 1))], route_r.at[1])

    def shuffle_b(n):
        send_b2[n] = recv_b1[first_ref[n]] + recv_b1[last_ref[n]]

    loop(devices, shuffle_b)
    route(3, send_b2, lambda m: recv_b2.at[m])
    recv_b2[me] = send_b2[me]
    loop(pairs, functools.partial(inner, 1))

    def outer_r(p):
        for i in range(2):
            state = recv_f2[pl.ds(p * dests, dests), i].reshape(HEAD, LANES)
            sd = tuple(block_diag(a) for a in split(state))
            rows = slice((i + 1) * T, (i + 2) * T)
            r = rkv_ref[0, i, :, lanes(p)].astype(F32)
            drs = ef[rows, lanes(p)] * right2(nt, dy_ref[i, :, lanes(p)], sd)
            rkv_out[0, i, :, lanes(p)] = (dr_loc[i, :, lanes(p)] + drs).astype(BF16)
            dd = right2(nn, suffix, split(r * drs)) + dd_loc[i, :, lanes(p)]
            dz_ref[rows, lanes(p)] = dd * dec[rows, lanes(p)]

    def outer_p(p):
        state = recv_b2[pl.ds(p * dests, dests)].reshape(HEAD, LANES)
        sd = tuple(block_diag(a) for a in split(state))
        e = ef[:T, lanes(p)]
        k = kv_ref[0, 0, :, lanes(p)].astype(F32)
        dk = e * right2(nt, kv_ref[1, 0, :, lanes(p)], sd)
        dv = dot3(nn, split(k * e), sd)
        kv_out[0, 0, :, lanes(p)] = dk.astype(BF16)
        kv_out[1, 0, :, lanes(p)] = dv.astype(BF16)
        dd = right2(nn, before, split(k * dk))
        dz_ref[:T, lanes(p)] = dd * dec[:T, lanes(p)]

    def dth_part(lo, hi, p, acc):
        return acc + dot3(nt, split(dz_ref[lo * T : hi * T, lanes(p)]), split(up_ref[:, lanes(p)]))

    bulk_wait(recv_f2.at[pl.ds(0, devices - 1)], route_r.at[2])
    loop(pairs, outer_r)
    dth_r_src[...] = loop(
        pairs, functools.partial(dth_part, 1, 3), jnp.zeros((2 * T, RANK), F32)
    )
    exchange(dth_r_src, dth_r_land, dth_r_s, dth_r_r)
    bulk_wait(recv_b2.at[pl.ds(0, devices - 1)], route_r.at[3])
    loop(pairs, outer_p)
    dth_p_src[...] = loop(pairs, functools.partial(dth_part, 0, 1), jnp.zeros((T, RANK), F32))
    exchange(dth_p_src, dth_p_land, dth_p_s, dth_p_r)
    store(rkv_out, rkv_hbm_out)
    store(kv_out, kv_hbm_out)

    place = [lax.rem(me // g, n) for g, n in stages]
    size = [channels]
    for g, n in stages:
        size.append(size[-1] // n)
    lands = (land0, land1, land2)
    sums = (cur1, cur2, cur3)

    def peers(stage):
        g, n = stages[stage]
        q = place[stage]
        for i in range(1, n):
            other = lax.rem(q + i, n)
            yield i, other, me + (other - q) * g

    def source(half, stage):
        return grad.at[half] if stage == 0 else sums[stage - 1].at[half]

    def rs_start(half, stage):
        rows = size[stage + 1]
        for i, other, peer in peers(stage):
            remote(
                source(half, stage).at[pl.ds(pl.multiple_of(other * rows, 8), rows)],
                lands[stage].at[half, place[stage]],
                rs_s.at[half, stage, i],
                rs_r.at[half, stage, place[stage]],
                "dp",
                peer,
            ).start()

    def rs_finish(half, stage):
        rows = size[stage + 1]
        total = source(half, stage)[pl.ds(pl.multiple_of(place[stage] * rows, 8), rows), :]
        for i, other, peer in peers(stage):
            bulk_wait(lands[stage].at[half, other], rs_r.at[half, stage, other])
            total = total + lands[stage][half, other]
        sums[stage][half] = total

    offs = [0]
    for stage in range(3):
        offs.append(offs[-1] + place[stage] * size[stage + 1])

    def piece(half, stage, q):
        rows = size[stage + 1]
        return fin.at[half, pl.ds(pl.multiple_of(offs[stage] + q * rows, 8), rows)]

    def ag_start(half, stage):
        if stage == 2:
            fin[half, pl.ds(pl.multiple_of(offs[3], 8), size[3]), :] = sums[2][half]
        q = place[stage]
        mine = piece(half, stage, q)
        for i, other, peer in peers(stage):
            ssem, rsem = ag_s.at[half, stage, i], ag_r.at[half, stage, q]
            remote(mine, mine, ssem, rsem, "dp", peer).start()

    def ag_finish(half, stage):
        for i, other, peer in peers(stage):
            bulk_wait(piece(half, stage, other), ag_r.at[half, stage, other])

    def vec_start(stage):
        q = place[stage]
        at = sum(m for _, m in stages[:stage])
        mine = vec.at[pl.ds(3 * stage, 3)]
        for i, other, peer in peers(stage):
            ssem, rsem = vec_s.at[stage, i], vec_r.at[stage, q]
            remote(mine, vec_land.at[at + q], ssem, rsem, "dp", peer).start()
        vec_land[at + q] = vec[3 * stage : 3 * stage + 3]

    def vec_finish(stage):
        at = sum(m for _, m in stages[:stage])
        for i, other, peer in peers(stage):
            bulk_wait(vec_land.at[at + other], vec_r.at[stage, other])
        total = vec_land[at]
        for i in range(1, stages[stage][1]):
            total = total + vec_land[at + i]
        if stage == 2:
            vec_out[...] = total
        else:
            vec[3 * stage + 3 : 3 * stage + 6] = total

    def dh_piece(stage, q):
        g = stages[stage][0]
        return dh_land.at[pl.ds(2 * (me - lax.rem(me, g) + (q - place[stage]) * g), 2 * g)]

    def dh_start(stage):
        q = place[stage]
        mine = dh_piece(stage, q)
        for i, other, peer in peers(stage):
            remote(mine, mine, dh_s.at[stage, i], dh_r.at[stage, q], "dp", peer).start()

    def dh_finish(stage):
        for i, other, peer in peers(stage):
            bulk_wait(dh_piece(stage, other), dh_r.at[stage, other])

    def up_grads(p):
        dz = dz_ref[:, lanes(p)]
        grad[0, rows_of(p), :] = dot3(tn, split(th_ref[...]), split(dz))
        vec[0, :, lanes(p)] = jnp.sum(dz, axis=0, keepdims=True)

    loop(pairs, up_grads)
    rs_start(0, 0)

    th = th_ref[T:, :]
    dh_ref[T:, :] = exchanged(dth_r_land, dth_r_r) * (1.0 - th * th)
    for i in range(2):
        dh_land[2 * me + i] = dh_ref[(i + 1) * T : (i + 1) * T + 1, :]
    dh_start(0)
    th = th_ref[:T, :]
    dh_ref[:T, :] = exchanged(dth_p_land, dth_p_r) * (1.0 - th * th)

    def down_grads(p):
        grad[1, rows_of(p), :] = dot3(tn, split(mixed[:, lanes(p)]), split(dh_ref[...]))

    loop(pairs, down_grads)
    rs_start(1, 0)

    def x_grads(p):
        f = f_ref[:, lanes(p)]
        dm = dot3(nt, split(dh_ref[...]), split(down_ref[rows_of(p), :]))
        mix_sum = jnp.zeros((1, LANES), F32)
        for i in range(3):
            x = x_of(i, p)
            g = dm[i * T : (i + 1) * T]
            ahead = jnp.where(last_row, 0.0, pltpu.roll(g, T - 1, 0))
            first = 0.0 if i == 0 else lead[i - 1 : i, lanes(p)]
            prev = jnp.where(first_row, first, pltpu.roll(x, 1, 0))
            dx = g + (ahead - g) * f
            mix_sum = mix_sum + jnp.sum(g * (prev - x), axis=0, keepdims=True)
            if i == 0:
                xp_out[0, :, lanes(p)] = dx.astype(BF16)
                xp_tail[:, lanes(p)] = dx[T - 16 :]
            else:
                xr_out[i - 1, :, lanes(p)] = dx.astype(BF16)
        vec[2, :, lanes(p)] = mix_sum

    def x_tail(late, p):
        f = f_ref[:, lanes(p)]
        more = f * dot3(nt, split(late), split(down_ref[rows_of(p), :]))[0:1]
        tail = xp_tail[:, lanes(p)]
        at_end = lax.broadcasted_iota(jnp.int32, (16, LANES), 0) == 15
        xp_out[0, T - 16 :, lanes(p)] = jnp.where(at_end, tail + more, tail).astype(BF16)

    rs_finish(0, 0)
    rs_start(0, 1)
    dh_finish(0)
    dh_start(1)
    loop(pairs, x_grads)
    vec_start(0)
    store(xr_out, xr_hbm_out)
    rs_finish(1, 0)
    rs_start(1, 1)
    rs_finish(0, 1)
    rs_start(0, 2)
    dh_finish(1)
    dh_start(2)
    vec_finish(0)
    vec_start(1)
    rs_finish(1, 1)
    rs_start(1, 2)
    rs_finish(0, 2)
    ag_start(0, 2)
    vec_finish(1)
    vec_start(2)
    rs_finish(1, 2)
    ag_start(1, 2)
    dh_finish(2)
    late = dh_land[first_ref[me]] + dh_land[last_ref[me]]
    loop(pairs, functools.partial(x_tail, jnp.broadcast_to(late, (8, RANK))))
    store(xp_out, xp_hbm_out)
    ag_finish(0, 2)
    ag_start(0, 1)
    vec_finish(2)
    store(vec_out, vec_hbm_out)
    ag_finish(1, 2)
    ag_start(1, 1)
    ag_finish(0, 1)
    ag_start(0, 0)
    ag_finish(1, 1)
    ag_start(1, 0)
    ag_finish(0, 0)
    store(fin.at[0], grad_hbm_out.at[0])
    ag_finish(1, 0)
    store(fin.at[1], grad_hbm_out.at[1])

    bulk_wait(row_land.at[pl.ds(0, devices - 1)], row_s)
    bulk_wait(recv_f1.at[pl.ds(0, devices - 1)], route_s.at[0])
    bulk_wait(recv_b1.at[pl.ds(0, 2 * (devices - 1))], route_s.at[1])
    bulk_wait(recv_f2.at[pl.ds(0, devices - 1)], route_s.at[2])
    bulk_wait(recv_b2.at[pl.ds(0, devices - 1)], route_s.at[3])
    for i in range(1, ranks):
        bulk_wait(hid_p_land.at[0], hid_p_s.at[i])
        bulk_wait(hid_r_land.at[0], hid_r_s.at[i])
        bulk_wait(lead_land.at[0], lead_s.at[i])
        bulk_wait(dth_r_land.at[0], dth_r_s.at[i])
        bulk_wait(dth_p_land.at[0], dth_p_s.at[i])
    for stage, (g, n) in enumerate(stages):
        for i in range(1, n):
            bulk_wait(vec_land.at[0], vec_s.at[stage, i])
            bulk_wait(dh_piece(stage, place[stage]), dh_s.at[stage, i])
            for half in range(2):
                bulk_wait(lands[stage].at[half, 0], rs_s.at[half, stage, i])
                bulk_wait(piece(half, stage, place[stage]), ag_s.at[half, stage, i])
    for copy in stores:
        copy.wait()


def results(pairs, *refs):
    sources, outs, held, (in_sem, out_sem) = refs[:6], refs[6:15], refs[15:21], refs[21:]
    loads = [
        pltpu.make_async_copy(a, b, in_sem.at[n]) for n, (a, b) in enumerate(zip(sources, held))
    ]
    for load in loads:
        load.start()
    moves = [[(held[n], outs[n])] for n in range(4)]
    moves.append([(held[4].at[1], outs[4])])
    for p in range(pairs):
        lanes = pl.ds(p * LANES, LANES)
        moves[4].append((held[4].at[0, lanes], outs[5].at[:, lanes]))
    moves.append([(held[5].at[n], outs[6 + n]) for n in range(3)])
    copies = []
    for load, group in zip(loads, moves):
        load.wait()
        for src, dst in group:
            copies.append(pltpu.make_async_copy(src, dst, out_sem.at[len(copies)]))
            copies[-1].start()
    for copy in copies:
        copy.wait()


def per_device(
    query_text_memory,
    query_text_feed,
    reply_acceptor_memory,
    reply_feed,
    reply_cotangent_vector,
    query_placement,
    reply_parent_query,
    fading_narrowing,
    fading_widening,
    fading_anchor_rate,
    self_emphasis,
    lagged_token_fraction,
):
    devices = lax.axis_size("dp")
    ranks = lax.axis_size("mp")
    channels = query_text_feed.shape[2]
    pairs = channels // LANES
    per = HEAD * pairs // devices
    responses = reply_parent_query.shape[0]
    matches = query_placement[None, :] == reply_parent_query[:, None]
    slots = jnp.arange(devices, dtype=jnp.int32)
    owner = jnp.sum(jnp.where(matches, slots[None, :], 0), axis=1).astype(jnp.int32)
    index = jnp.arange(responses, dtype=jnp.int32)[:, None]
    first = jnp.min(jnp.where(matches, index, responses - 1), axis=0)
    last = jnp.max(jnp.where(matches, index, 0), axis=0)
    stages = stages_of(devices)
    size = [channels]
    for g, n in stages:
        size.append(size[-1] // n)

    def vmem(*shape, dtype=F32):
        return pltpu.VMEM(shape, dtype)

    operands = (
        query_text_memory,
        query_text_feed,
        reply_acceptor_memory,
        reply_feed,
        reply_cotangent_vector,
        fading_narrowing,
        fading_widening,
        fading_anchor_rate[None],
        self_emphasis[None],
        lagged_token_fraction[None],
    )
    dma = pltpu.SemaphoreType.DMA
    shapes = [
        jax.ShapeDtypeStruct(a.shape, BF16)
        for a in (reply_acceptor_memory, reply_feed, query_text_memory, query_text_feed)
    ]
    scratch = [pltpu.VMEM(a.shape, a.dtype) for a in shapes]
    scratch += [vmem(3, 1, channels)]
    scratch += [pltpu.VMEM(a.shape, a.dtype) for a in operands]
    scratch += [
        vmem((len(LEVELS) + 1) * T, T, dtype=BF16),
        vmem(T, len(LEVELS) * T, dtype=BF16),
        vmem(len(LEVELS) * T, LANES),
        vmem(1, channels),
        vmem(devices, 1, channels),
        vmem(3 * T, channels),
        vmem(T, RANK),
        vmem(ranks, T, RANK),
        vmem(2 * T, RANK),
        vmem(ranks, 2 * T, RANK),
        vmem(8, channels),
        vmem(8, RANK),
        vmem(ranks, 8, RANK),
        vmem(3 * T, channels),
        vmem(3 * T, channels),
        vmem(devices, per, LANES),
        vmem(devices, per, LANES),
        vmem(devices, 2, per, LANES),
        vmem(2 * devices, per, LANES),
        vmem(devices, 2, per, LANES),
        vmem(devices, 2, per, LANES),
        vmem(devices, per, LANES),
        vmem(devices, per, LANES),
        vmem(2, T, channels),
        vmem(2, T, channels),
        vmem(3 * T, RANK),
        vmem(3 * T, channels),
        vmem(2 * T, RANK),
        vmem(ranks, 2 * T, RANK),
        vmem(T, RANK),
        vmem(ranks, T, RANK),
        vmem(3 * T, RANK),
        vmem(2 * devices, 1, RANK),
        vmem(16, channels),
        vmem(9, 1, channels),
        vmem(sum(n for _, n in stages), 3, 1, channels),
        vmem(2, channels, RANK),
        vmem(2, size[1], RANK),
        vmem(2, size[2], RANK),
        vmem(2, size[3], RANK),
        vmem(2, stages[0][1], size[1], RANK),
        vmem(2, stages[1][1], size[2], RANK),
        vmem(2, stages[2][1], size[3], RANK),
        vmem(2, channels, RANK),
        dma((len(operands),)),
        dma((7,)),
        dma,
        dma,
        dma((ranks,)),
        dma((ranks,)),
        dma((ranks,)),
        dma((ranks,)),
        dma((ranks,)),
        dma((ranks,)),
        dma((4,)),
        dma((4,)),
        dma((ranks,)),
        dma((ranks,)),
        dma((ranks,)),
        dma((ranks,)),
        dma((3, 8)),
        dma((3, 8)),
        dma((3, 8)),
        dma((3, 8)),
        dma((2, 3, 8)),
        dma((2, 3, 8)),
        dma((2, 3, 8)),
        dma((2, 3, 8)),
    ]
    scalars = pl.BlockSpec(memory_space=pltpu.SMEM)
    far = pl.BlockSpec(memory_space=pltpu.HBM)
    moved = pl.pallas_call(
        functools.partial(body, devices, ranks, channels),
        out_shape=(
            *shapes,
            jax.ShapeDtypeStruct((2, channels, RANK), F32),
            jax.ShapeDtypeStruct((3, 1, channels), F32),
        ),
        in_specs=[scalars] * 3 + [far] * len(operands),
        out_specs=[far] * 6,
        scratch_shapes=scratch,
        compiler_params=pltpu.CompilerParams(
            collective_id=0, has_side_effects=True, vmem_limit_bytes=VMEM
        ),
    )(owner, first, last, *operands)
    rkv, xr, kv, xp, down, up, *vectors = pl.pallas_call(
        functools.partial(results, pairs),
        out_shape=(
            *shapes,
            jax.ShapeDtypeStruct(fading_narrowing.shape, F32),
            jax.ShapeDtypeStruct(fading_widening.shape, F32),
            *[jax.ShapeDtypeStruct((1, channels), F32)] * 3,
        ),
        in_specs=[far] * 6,
        out_specs=[far] * 9,
        scratch_shapes=[pltpu.VMEM(a.shape, a.dtype) for a in moved]
        + [dma((6,)), dma((8 + pairs,))],
        compiler_params=pltpu.CompilerParams(vmem_limit_bytes=VMEM),
    )(*moved)
    return rkv, xr, kv, xp, down, up, *[v.reshape(channels) for v in vectors]


def solution(mesh):
    in_specs = (
        P(None, "dp", None, "mp"),
        P("dp", None, "mp"),
        P(None, "dp", None, "mp"),
        P("dp", None, "mp"),
        P("dp", None, "mp"),
        P(),
        P(),
        P("mp", None),
        P(None, "mp"),
        P("mp"),
        P("mp"),
        P("mp"),
    )
    out_specs = (
        P(None, "dp", None, "mp"),
        P("dp", None, "mp"),
        P(None, "dp", None, "mp"),
        P("dp", None, "mp"),
        P("mp", None),
        P(None, "mp"),
        P("mp"),
        P("mp"),
        P("mp"),
    )
    return jax.shard_map(
        per_device, mesh=mesh, in_specs=in_specs, out_specs=out_specs, check_vma=False
    )
```

time: 143 us -> 111 us (0.78)
  Pallas kernels: 126 us -> 108 us
  local copies, waits for them, and re-layouts: 14.7 us -> 0.66 us
    pallas_call x1, Pallas kernels: 126 us -> 106 us  [per_device(): pl.pallas_call(functools.partial(body, devices, ranks, channels), out_sha...]
    unnamed x32 -> x4, local copies, waits for them, and re-layouts: 13.9 us -> 0.66 us
    pallas_call x0 -> x1, Pallas kernels: none -> 2.81 us  [per_device(): pl.pallas_call(functools.partial(results, pairs), out_shape=(*shapes, jax...]
where the time goes in v2:
time: 111 us; the launch traced here: 110 us
  Pallas kernels  108 us (97%)
    pallas_call x1, Pallas kernels, per_device(): pl.pallas_call(functools.partial(body, devices, ranks, channels), out_sha...  106 us
    pallas_call x1, Pallas kernels, per_device(): pl.pallas_call(functools.partial(results, pairs), out_shape=(*shapes, jax...  2.81 us

profile of v2, /device:TPU:1, one launch (start us, length us, event | category | flops | bytes accessed | tf_op | source)
XLA Modules:
  0.0 110.4 jit_solution(3840999372196060447)
XLA Ops:
  0.6 0.0 copy-start
  0.7 0.0 copy-start.1
  0.7 0.6 copy-done
  1.3 0.0 copy-done.1
  1.3 0.7 fusion.2
  2.0 105.6 %shard_map.187 = (bf16[3,2,64,1024]{3,2,1,0:T(8,128)(2,1)}, bf16[2,64,1024]{2,1,0:T(8,128)(2,1)}, bf16[2,1,64,1024]{3,2,1,0:T(8,128)(2,1)}, bf16[1,64,1024]{2,1,...) custom-call(s32[128]{0:T(128)} %get-tuple-element.41.owner_ref, s32[64]{0:T(128)} %get-tuple-element.40.first_ref, ...), custom_call_target="tpu_custom_call" | custom-call | tf_op jit(solution)/shard_map/pallas_call | solution.py:853
  107.6 2.8 %shard_map.188 = (bf16[3,2,64,1024]{3,2,1,0:T(8,128)(2,1)}, bf16[2,64,1024]{2,1,0:T(8,128)(2,1)}, bf16[2,1,64,1024]{3,2,1,0:T(8,128)(2,1)}, bf16[1,64,1024]{2,1,...) custom-call(bf16[3,2,64,1024]{3,2,1,0:T(8,128)(2,1)} %get-tuple-elem, ...), custom_call_target="tpu_custom_call" | custom-call | tf_op jit(solution)/shard_map/pallas_call | solution.py:867
Async XLA Ops:
  0.6 0.7 copy-start
  0.7 0.7 copy-start.1

commit v3 on v2

v3 whole, which is shorter than its diff:
```python
import functools

import jax
import jax.numpy as jnp
from jax import lax
from jax.experimental import pallas as pl
from jax.experimental.pallas import tpu as pltpu
from jax.sharding import PartitionSpec as P

HEAD = 64
T = 64
LANES = 128
RANK = 128
VMEM = 63 * 1024 * 1024
LEVELS = (32, 16, 8, 4, 2, 1)
MESH = pl.DeviceIdType.MESH
F32 = jnp.float32
BF16 = jnp.bfloat16


def stages_of(devices):
    if devices == 64:
        return ((1, 2), (2, 4), (8, 8))
    return ((1, 2), (2, 2), (4, devices // 4))


def nn(a, b):
    return lax.dot_general(a, b, (((1,), (0,)), ((), ())), preferred_element_type=F32)


def nt(a, b):
    return lax.dot_general(a, b, (((1,), (1,)), ((), ())), preferred_element_type=F32)


def tn(a, b):
    return lax.dot_general(a, b, (((0,), (0,)), ((), ())), preferred_element_type=F32)


def split(x):
    hi = x.astype(BF16)
    return hi, (x - hi.astype(F32)).astype(BF16)


def split3(x):
    hi = x.astype(BF16)
    rest = x - hi.astype(F32)
    mid = rest.astype(BF16)
    return hi, mid, (rest - mid.astype(F32)).astype(BF16)


def dot3(dot, a, b):
    return dot(a[0], b[0]) + (dot(a[0], b[1]) + dot(a[1], b[0]))


def left2(dot, a, b):
    return dot(a[0], b) + dot(a[1], b)


def right2(dot, a, b):
    return dot(a, b[0]) + dot(a, b[1])


def block_diag(x):
    head = lax.broadcasted_iota(jnp.int32, x.shape, 1) // HEAD
    zero = jnp.zeros_like(x)
    return jnp.concatenate(
        [jnp.where(head == h, x, zero) for h in range(x.shape[1] // HEAD)], axis=0
    )


def pack_diag(m):
    n = m.shape[1] // HEAD
    head = lax.broadcasted_iota(jnp.int32, (HEAD, m.shape[1]), 1) // HEAD
    out = m[:HEAD]
    for h in range(1, n):
        out = jnp.where(head == h, m[h * HEAD : (h + 1) * HEAD], out)
    return out


def body(
    devices,
    ranks,
    channels,
    place_hbm,
    parent_hbm,
    kv_hbm,
    xp_hbm,
    rkv_hbm,
    xr_hbm,
    dy_hbm,
    down_hbm,
    up_hbm,
    base_hbm,
    u_hbm,
    f_hbm,
    rkv_hbm_out,
    xr_hbm_out,
    kv_hbm_out,
    xp_hbm_out,
    grad_hbm_out,
    vec_hbm_out,
    rkv_out,
    xr_out,
    kv_out,
    xp_out,
    vec_out,
    place_ref,
    parent_ref,
    kv_ref,
    xp_ref,
    rkv_ref,
    xr_ref,
    dy_ref,
    down_ref,
    up_ref,
    base_ref,
    u_ref,
    f_ref,
    owner_vec,
    first_vec,
    last_vec,
    owner_ref,
    first_ref,
    last_ref,
    gaps_ref,
    gaps_t_ref,
    masks_ref,
    row_src,
    row_land,
    mixed,
    hid_p,
    hid_p_land,
    hid_r,
    hid_r_land,
    lead,
    lead_hid,
    lead_land,
    dec,
    ef,
    send_f1,
    recv_f1,
    send_b1,
    recv_b1,
    send_f2,
    recv_f2,
    send_b2,
    recv_b2,
    dr_loc,
    dd_loc,
    th_ref,
    dz_ref,
    dth_r_src,
    dth_r_land,
    dth_p_src,
    dth_p_land,
    dh_ref,
    dh_land,
    xp_tail,
    vec,
    vec_land,
    grad,
    cur1,
    cur2,
    cur3,
    land0,
    land1,
    land2,
    fin,
    in_sem,
    index_sem,
    out_sem,
    row_s,
    row_r,
    hid_p_s,
    hid_p_r,
    hid_r_s,
    hid_r_r,
    lead_s,
    lead_r,
    route_s,
    route_r,
    dth_r_s,
    dth_r_r,
    dth_p_s,
    dth_p_r,
    dh_s,
    dh_r,
    vec_s,
    vec_r,
    rs_s,
    rs_r,
    ag_s,
    ag_r,
):
    me = lax.axis_index("dp")
    rank = lax.axis_index("mp")
    wide = min(2 * LANES, channels)
    blocks = wide // LANES
    steps = channels // wide
    per = HEAD * (channels // LANES) // devices
    dests = HEAD // per
    stages = stages_of(devices)

    def lanes(p):
        return pl.ds(pl.multiple_of(p * wide, LANES), wide)

    rows_of = lanes

    def loop(n, fn, init=None):
        if init is None:
            lax.fori_loop(0, n, lambda i, c: (fn(i), c)[1], 0)
            return None
        return lax.fori_loop(0, n, fn, init)

    def remote(src, dst, ssem, rsem, axis, peer):
        return pltpu.make_async_remote_copy(
            src_ref=src,
            dst_ref=dst,
            send_sem=ssem,
            recv_sem=rsem,
            device_id={axis: peer},
            device_id_type=MESH,
        )

    def bulk_wait(view, sem):
        pltpu.make_async_copy(view, view, sem).wait()

    pending = []

    barrier = pltpu.get_barrier_semaphore()

    def greet(i):
        pl.semaphore_signal(
            barrier, inc=1, device_id={"dp": lax.rem(me + 1 + i, devices)}, device_id_type=MESH
        )

    fetches = [
        pltpu.make_async_copy(src, dst, in_sem.at[n])
        for n, (src, dst) in enumerate(
            (
                (xp_hbm, xp_ref),
                (xr_hbm, xr_ref),
                (f_hbm, f_ref),
                (down_hbm, down_ref),
                (up_hbm, up_ref),
                (base_hbm, base_ref),
                (kv_hbm, kv_ref),
                (rkv_hbm, rkv_ref),
                (dy_hbm, dy_ref),
                (u_hbm, u_ref),
                (place_hbm, place_ref),
                (parent_hbm, parent_ref),
            )
        )
    ]
    for fetch in fetches:
        fetch.start()

    for i in range(1, ranks):
        pl.semaphore_signal(
            barrier, inc=1, device_id={"mp": lax.rem(rank + i, ranks)}, device_id_type=MESH
        )
    loop(devices - 1, greet)

    stores = []

    def store(src, dst):
        copy = pltpu.make_async_copy(src, dst, out_sem.at[len(stores)])
        copy.start()
        stores.append(copy)

    first_row = lax.broadcasted_iota(jnp.int32, (T, wide), 0) == 0
    last_row = lax.broadcasted_iota(jnp.int32, (T, wide), 0) == T - 1

    def x_of(i, p):
        return (xp_ref[0, :, lanes(p)] if i == 0 else xr_ref[i - 1, :, lanes(p)]).astype(F32)

    def mix(p, acc):
        f = f_ref[:, lanes(p)]
        parts = []
        for i in range(3):
            x = x_of(i, p)
            prev = jnp.where(first_row, 0.0, pltpu.roll(x, 1, 0))
            m = x + (prev - x) * f
            mixed[i * T : (i + 1) * T, lanes(p)] = m
            parts.append(m)
        return acc + dot3(nn, split(jnp.concatenate(parts, axis=0)), split(down_ref[rows_of(p), :]))

    for fetch in fetches[:4]:
        fetch.wait()
    row_src[...] = xp_ref[0, T - 16 :, :].astype(F32)[15:16]
    partial = loop(steps, mix, jnp.zeros((3 * T, RANK), F32))
    hid_p[...] = partial[:T]
    hid_r[...] = partial[T:]
    for fetch in fetches[4:]:
        fetch.wait()
    pl.semaphore_wait(barrier, devices - 1 + ranks - 1)

    def exchange(src, land, ssem, rsem):
        for i in range(1, ranks):
            peer = lax.rem(rank + i, ranks)
            remote(src, land.at[rank], ssem.at[i], rsem.at[rank], "mp", peer).start()
            pending.append((src, ssem.at[i]))
        land[rank] = src[...]

    def exchanged(land, rsem):
        for i in range(1, ranks):
            source = lax.rem(rank + i, ranks)
            bulk_wait(land.at[source], rsem.at[source])
        total = land[0]
        for i in range(1, ranks):
            total = total + land[i]
        return total

    def send_row(i):
        peer = lax.rem(me + 1 + i, devices)
        remote(row_src, row_land.at[me], row_s, row_r, "dp", peer).start()

    exchange(hid_p, hid_p_land, hid_p_s, hid_p_r)
    loop(devices - 1, send_row)
    pending.append((row_land.at[pl.ds(0, devices - 1)], row_s))
    row_land[me] = row_src[...]
    exchange(hid_r, hid_r_land, hid_r_s, hid_r_r)
    t_sq = lax.broadcasted_iota(jnp.int32, (T, T), 0)
    j_sq = lax.broadcasted_iota(jnp.int32, (T, T), 1)
    before = (j_sq < t_sq).astype(F32).astype(BF16)
    suffix = (j_sq > t_sq).astype(F32).astype(BF16)

    def exact(mask, x):
        hi, mid, low = split3(x)
        return nn(mask, hi) + (nn(mask, mid) + nn(mask, low))

    def decays(lo, hi, p):
        z = dot3(nn, split(th_ref[lo * T : hi * T, :]), split(up_ref[:, lanes(p)]))
        d = -jnp.exp(z + base_ref[:, lanes(p)])
        dec[lo * T : hi * T, lanes(p)] = d
        for i in range(lo, hi):
            at = (i - lo) * T
            e = jnp.exp(exact(suffix if i == 0 else before, d[at : at + T]))
            ef[i * T : (i + 1) * T, lanes(p)] = e
            if i == 0:
                a, b = kv_ref[0, 0, :, lanes(p)], kv_ref[1, 0, :, lanes(p)]
            else:
                a, b = rkv_ref[0, i - 1, :, lanes(p)], dy_ref[i - 1, :, lanes(p)]
            packed = pack_diag(left2(tn, split(a.astype(F32) * e), b))
            for n in range(blocks):
                part = packed[:, n * LANES : (n + 1) * LANES].reshape(dests, per, LANES)
                at = pl.ds((p * blocks + n) * dests, dests)
                if i == 0:
                    send_f1[at] = part
                else:
                    send_b1[at, i - 1] = part

    def route(n, src, dst_of):
        def send(i):
            peer = lax.rem(me + 1 + i, devices)
            remote(src.at[peer], dst_of(me), route_s.at[n], route_r.at[n], "dp", peer).start()

        loop(devices - 1, send)
        pending.append((src.at[pl.ds(0, devices - 1)], route_s.at[n]))

    def column(row):
        n = row.shape[1]
        diagonal = lax.broadcasted_iota(jnp.int32, (n, n), 0) == lax.broadcasted_iota(
            jnp.int32, (n, n), 1
        )
        return jnp.sum(jnp.where(diagonal, row, 0), axis=1, keepdims=True)

    placed, parents = place_ref[...], parent_ref[...]
    pairs_at = (devices, 2 * devices)
    match = column(placed) == parents
    slot = lax.broadcasted_iota(jnp.int32, pairs_at, 0)
    owner_vec[...] = jnp.max(jnp.where(match, slot, 0), axis=0, keepdims=True)
    match = column(parents) == placed
    response = lax.broadcasted_iota(jnp.int32, pairs_at[::-1], 0)
    first_vec[...] = jnp.min(
        jnp.where(match, response, 2 * devices - 1), axis=0, keepdims=True
    )
    last_vec[...] = jnp.max(jnp.where(match, response, 0), axis=0, keepdims=True)
    indices = [
        pltpu.make_async_copy(src, dst, index_sem.at[n])
        for n, (src, dst) in enumerate(
            ((owner_vec, owner_ref), (first_vec, first_ref), (last_vec, last_ref))
        )
    ]
    for copy in indices:
        copy.start()
    for copy in indices:
        copy.wait()

    def gap_mask(shape, t_axis, level):
        t = lax.broadcasted_iota(jnp.int32, shape, t_axis)
        j = lax.broadcasted_iota(jnp.int32, shape, 1 - t_axis)
        b = LEVELS[level]
        second = (t & b) != 0
        late = second & (j >= (t & -b)) & (j < t)
        early = ~second & (j > t) & (j <= (t | (b - 1)))
        return (late | early).astype(F32).astype(BF16)

    for level in range(len(LEVELS)):
        gaps_ref[level * T : (level + 1) * T, :] = gap_mask((T, T), 0, level)
    for level in range(0, len(LEVELS), 2):
        both = [gap_mask((T, T), 1, level + n) for n in range(2)]
        gaps_t_ref[:, level * T : (level + 2) * T] = jnp.concatenate(both, axis=1)
    t_row = lax.broadcasted_iota(jnp.int32, (T, wide), 0)
    s_col = lax.broadcasted_iota(jnp.int32, (T, wide), 1) & (T - 1)
    apart = t_row ^ s_col
    for level, b in enumerate(LEVELS):
        masks_ref[level * T : (level + 1) * T, :] = ((apart >= b) & (apart < 2 * b)).astype(F32)

    th_ref[:T, :] = jnp.tanh(exchanged(hid_p_land, hid_p_r))
    loop(steps, functools.partial(decays, 0, 1))
    bulk_wait(row_land.at[pl.ds(0, devices - 1)], row_r)
    lead_rows = [row_land[owner_ref[0, 2 * me + i]] for i in range(2)]
    row8 = lax.broadcasted_iota(jnp.int32, (8, channels), 0)
    lead[...] = jnp.where(row8 == 0, lead_rows[0], jnp.where(row8 == 1, lead_rows[1], 0.0))

    def lead_mix(p, acc):
        fl = f_ref[:, lanes(p)] * lead[:, lanes(p)]
        for i in range(2):
            at = (i + 1) * T
            mixed[at : at + 1, lanes(p)] = mixed[at : at + 1, lanes(p)] + fl[i : i + 1]
        return acc + dot3(nn, split(fl), split(down_ref[rows_of(p), :]))

    lead_hid[...] = loop(steps, lead_mix, jnp.zeros((8, RANK), F32))
    exchange(lead_hid, lead_land, lead_s, lead_r)
    route(0, send_f1, lambda m: recv_f1.at[m])
    recv_f1[me] = send_f1[me]

    hidden = exchanged(hid_r_land, hid_r_r)
    th_ref[T:, :] = jnp.tanh(hidden)
    extra = exchanged(lead_land, lead_r)
    for i in range(2):
        at = (i + 1) * T
        th_ref[at : at + 1, :] = jnp.tanh(hidden[i * T : i * T + 1] + extra[i : i + 1])
    loop(steps, functools.partial(decays, 1, 3))
    route(1, send_b1, lambda m: recv_b1.at[pl.ds(2 * m, 2)])
    recv_b1[pl.ds(2 * me, 2)] = send_b1[me]

    bulk_wait(recv_f1.at[pl.ds(0, devices - 1)], route_r.at[0])

    def shuffle_f(n):
        send_f2[n, 0] = recv_f1[owner_ref[0, 2 * n]]
        send_f2[n, 1] = recv_f1[owner_ref[0, 2 * n + 1]]

    loop(devices, shuffle_f)
    route(2, send_f2, lambda m: recv_f2.at[m])
    recv_f2[me] = send_f2[me]

    ones_block = (
        (
            lax.broadcasted_iota(jnp.int32, (wide, wide), 0) // HEAD
            == lax.broadcasted_iota(jnp.int32, (wide, wide), 1) // HEAD
        )
        .astype(F32)
        .astype(BF16)
    )
    deep = len(LEVELS) - 1

    def inner(i, p):
        cols = lanes(p)
        rb, kb, vb = (rkv_ref[n, i, :, cols] for n in range(3))
        yb = dy_ref[i, :, cols]
        r, k, v, y = (a.astype(F32) for a in (rb, kb, vb, yb))
        d = dec[(i + 1) * T : (i + 2) * T, cols]
        u = u_ref[:, cols]
        y_diag = block_diag(yb)
        sym = jnp.where(t_row > s_col, nt(yb, block_diag(vb)), nt(vb, y_diag))
        gap = exact(gaps_ref[: deep * T, :], d)
        att = jnp.zeros((T, wide), F32)
        dr = jnp.zeros((T, wide), F32)
        dk = jnp.zeros((T, wide), F32)
        dgaps = []
        for level, b in enumerate(LEVELS):
            second = (t_row & b) != 0
            mask = masks_ref[level * T : (level + 1) * T, :]
            side = jnp.where(second, r, k)
            if level == deep:
                w = side.astype(BF16)
                wd = block_diag(w)
                att = att + mask * nt(w, wd)
                g = left2(nn, split(mask * sym), wd)
            else:
                x = jnp.exp(gap[level * T : (level + 1) * T])
                w = side * x
                ws = split(w)
                wd = tuple(block_diag(a) for a in ws)
                att = att + mask * dot3(nt, ws, wd)
                dw = dot3(nn, split(mask * sym), wd)
                dgaps.append(w * dw)
                g = x * dw
            dr = dr + jnp.where(second, g, 0.0)
            dk = dk + jnp.where(second, 0.0, g)
        dgap = jnp.concatenate(dgaps, axis=0)
        dd_loc[i, :, cols] = right2(nn, gaps_t_ref[:, : deep * T], split(dgap))
        self_a = left2(nn, split(r * u * k), ones_block)
        self_b = left2(nn, split(y * v), ones_block)
        dv = left2(nn, split(jnp.where(s_col > t_row, att, 0.0)), y_diag) + self_a * y
        dr_loc[i, :, cols] = dr + u * k * self_b
        rkv_out[1, i, :, cols] = (dk + u * r * self_b).astype(BF16)
        rkv_out[2, i, :, cols] = dv.astype(BF16)
        part = jnp.sum(r * k * self_b, axis=0, keepdims=True)
        if i == 0:
            vec[1, :, cols] = part
        else:
            vec[1, :, cols] = vec[1, :, cols] + part

    loop(steps, functools.partial(inner, 0))
    bulk_wait(recv_b1.at[pl.ds(0, 2 * (devices - 1))], route_r.at[1])

    def shuffle_b(n):
        send_b2[n] = recv_b1[first_ref[0, n]] + recv_b1[last_ref[0, n]]

    loop(devices, shuffle_b)
    route(3, send_b2, lambda m: recv_b2.at[m])
    recv_b2[me] = send_b2[me]
    loop(steps, functools.partial(inner, 1))

    def landed(ref, p, *i):
        parts = [
            ref[(pl.ds((p * blocks + n) * dests, dests), *i)].reshape(HEAD, LANES)
            for n in range(blocks)
        ]
        return tuple(block_diag(a) for a in split(jnp.concatenate(parts, axis=1)))

    def outer_r(p):
        for i in range(2):
            sd = landed(recv_f2, p, i)
            rows = slice((i + 1) * T, (i + 2) * T)
            r = rkv_ref[0, i, :, lanes(p)].astype(F32)
            drs = ef[rows, lanes(p)] * right2(nt, dy_ref[i, :, lanes(p)], sd)
            rkv_out[0, i, :, lanes(p)] = (dr_loc[i, :, lanes(p)] + drs).astype(BF16)
            dd = right2(nn, suffix, split(r * drs)) + dd_loc[i, :, lanes(p)]
            dz_ref[rows, lanes(p)] = dd * dec[rows, lanes(p)]

    def outer_p(p):
        sd = landed(recv_b2, p)
        e = ef[:T, lanes(p)]
        k = kv_ref[0, 0, :, lanes(p)].astype(F32)
        dk = e * right2(nt, kv_ref[1, 0, :, lanes(p)], sd)
        dv = dot3(nn, split(k * e), sd)
        kv_out[0, 0, :, lanes(p)] = dk.astype(BF16)
        kv_out[1, 0, :, lanes(p)] = dv.astype(BF16)
        dd = right2(nn, before, split(k * dk))
        dz_ref[:T, lanes(p)] = dd * dec[:T, lanes(p)]

    def dth_part(lo, hi, p, acc):
        return acc + dot3(nt, split(dz_ref[lo * T : hi * T, lanes(p)]), split(up_ref[:, lanes(p)]))

    bulk_wait(recv_f2.at[pl.ds(0, devices - 1)], route_r.at[2])
    loop(steps, outer_r)
    dth_r_src[...] = loop(
        steps, functools.partial(dth_part, 1, 3), jnp.zeros((2 * T, RANK), F32)
    )
    exchange(dth_r_src, dth_r_land, dth_r_s, dth_r_r)
    bulk_wait(recv_b2.at[pl.ds(0, devices - 1)], route_r.at[3])
    loop(steps, outer_p)
    dth_p_src[...] = loop(steps, functools.partial(dth_part, 0, 1), jnp.zeros((T, RANK), F32))
    exchange(dth_p_src, dth_p_land, dth_p_s, dth_p_r)
    store(rkv_out, rkv_hbm_out)
    store(kv_out, kv_hbm_out)

    place = [lax.rem(me // g, n) for g, n in stages]
    size = [channels // 2]
    for g, n in stages:
        size.append(size[-1] // n)
    lands = (land0, land1, land2)
    sums = (cur1, cur2, cur3)

    def peers(stage):
        g, n = stages[stage]
        q = place[stage]
        for i in range(1, n):
            other = lax.rem(q + i, n)
            yield i, other, me + (other - q) * g

    def addend(stream, stage, q):
        rows = size[stage + 1]
        ref, base = (grad, stream * size[0]) if stage == 0 else (sums[stage - 1].at[stream], 0)
        return ref.at[pl.ds(pl.multiple_of(base + q * rows, 8), rows)]

    def rs_start(stream, stage):
        for i, other, peer in peers(stage):
            part = addend(stream, stage, other)
            ssem, rsem = rs_s.at[stream, stage, i], rs_r.at[stream, stage, place[stage]]
            remote(part, lands[stage].at[stream, place[stage]], ssem, rsem, "dp", peer).start()
            pending.append((part, ssem))

    def rs_finish(stream, stage):
        total = addend(stream, stage, place[stage])[...]
        for i, other, peer in peers(stage):
            bulk_wait(lands[stage].at[stream, other], rs_r.at[stream, stage, other])
            total = total + lands[stage][stream, other]
        sums[stage][stream] = total

    offs = [0]
    for stage in range(3):
        offs.append(offs[-1] + place[stage] * size[stage + 1])

    def piece(stream, stage, q):
        rows = size[stage + 1]
        at = stream * size[0] + offs[stage] + q * rows
        return fin.at[pl.ds(pl.multiple_of(at, 8), rows)]

    def ag_start(stream, stage):
        q = place[stage]
        mine = piece(stream, stage, q)
        if stage == 2:
            mine[...] = sums[2][stream]
        for i, other, peer in peers(stage):
            ssem, rsem = ag_s.at[stream, stage, i], ag_r.at[stream, stage, q]
            remote(mine, mine, ssem, rsem, "dp", peer).start()
            pending.append((mine, ssem))

    def ag_finish(stream, stage):
        for i, other, peer in peers(stage):
            bulk_wait(piece(stream, stage, other), ag_r.at[stream, stage, other])

    def advance(stream, step):
        if step < 3:
            rs_finish(stream, step)
        else:
            ag_finish(stream, 5 - step)
        if step < 2:
            rs_start(stream, step + 1)
        elif step < 5:
            ag_start(stream, 4 - step)
        else:
            rows = pl.ds(stream * size[0], size[0])
            store(fin.at[rows], grad_hbm_out.at[rows])

    def vec_start(stage):
        q = place[stage]
        at = sum(m for _, m in stages[:stage])
        mine = vec.at[pl.ds(3 * stage, 3)]
        for i, other, peer in peers(stage):
            ssem, rsem = vec_s.at[stage, i], vec_r.at[stage, q]
            remote(mine, vec_land.at[at + q], ssem, rsem, "dp", peer).start()
            pending.append((mine, ssem))
        vec_land[at + q] = vec[3 * stage : 3 * stage + 3]

    def vec_finish(stage):
        at = sum(m for _, m in stages[:stage])
        for i, other, peer in peers(stage):
            bulk_wait(vec_land.at[at + other], vec_r.at[stage, other])
        total = vec_land[at]
        for i in range(1, stages[stage][1]):
            total = total + vec_land[at + i]
        if stage == 2:
            vec_out[...] = total
        else:
            vec[3 * stage + 3 : 3 * stage + 6] = total

    def dh_piece(stage, q):
        g = stages[stage][0]
        return dh_land.at[pl.ds(2 * (me - lax.rem(me, g) + (q - place[stage]) * g), 2 * g)]

    def dh_start(stage):
        q = place[stage]
        mine = dh_piece(stage, q)
        for i, other, peer in peers(stage):
            remote(mine, mine, dh_s.at[stage, i], dh_r.at[stage, q], "dp", peer).start()
            pending.append((mine, dh_s.at[stage, i]))

    def dh_finish(stage):
        for i, other, peer in peers(stage):
            bulk_wait(dh_piece(stage, other), dh_r.at[stage, other])

    def up_grads(p):
        dz = dz_ref[:, lanes(p)]
        g = dot3(tn, split(th_ref[...]), split(dz))
        for n in range(blocks):
            rows = pl.ds(pl.multiple_of(p * wide + n * LANES, LANES), LANES)
            grad[rows, :] = g[:, n * LANES : (n + 1) * LANES]
        vec[0, :, lanes(p)] = jnp.sum(dz, axis=0, keepdims=True)

    def down_grads(p):
        rows = pl.ds(pl.multiple_of(channels + p * wide, LANES), wide)
        grad[rows, :] = dot3(tn, split(mixed[:, lanes(p)]), split(dh_ref[...]))

    def both_streams(stream, fn):
        half = (steps + 1) // 2
        loop(half, fn)
        rs_start(stream, 0)
        loop(steps - half, lambda p: fn(p + half))
        rs_start(stream + 1, 0)

    both_streams(0, up_grads)

    th = th_ref[T:, :]
    dh_ref[T:, :] = exchanged(dth_r_land, dth_r_r) * (1.0 - th * th)
    for i in range(2):
        dh_land[2 * me + i] = dh_ref[(i + 1) * T : (i + 1) * T + 1, :]
    dh_start(0)
    advance(0, 0)
    advance(1, 0)
    th = th_ref[:T, :]
    dh_ref[:T, :] = exchanged(dth_p_land, dth_p_r) * (1.0 - th * th)
    both_streams(2, down_grads)

    def x_grads(p):
        f = f_ref[:, lanes(p)]
        dm = dot3(nt, split(dh_ref[...]), split(down_ref[rows_of(p), :]))
        mix_sum = jnp.zeros((1, wide), F32)
        for i in range(3):
            x = x_of(i, p)
            g = dm[i * T : (i + 1) * T]
            ahead = jnp.where(last_row, 0.0, pltpu.roll(g, T - 1, 0))
            first = 0.0 if i == 0 else lead[i - 1 : i, lanes(p)]
            prev = jnp.where(first_row, first, pltpu.roll(x, 1, 0))
            dx = g + (ahead - g) * f
            mix_sum = mix_sum + jnp.sum(g * (prev - x), axis=0, keepdims=True)
            if i == 0:
                xp_out[0, :, lanes(p)] = dx.astype(BF16)
                xp_tail[:, lanes(p)] = dx[T - 16 :]
            else:
                xr_out[i - 1, :, lanes(p)] = dx.astype(BF16)
        vec[2, :, lanes(p)] = mix_sum

    def x_tail(late, p):
        f = f_ref[:, lanes(p)]
        more = f * dot3(nt, split(late), split(down_ref[rows_of(p), :]))[0:1]
        tail = xp_tail[:, lanes(p)]
        at_end = lax.broadcasted_iota(jnp.int32, (16, wide), 0) == 15
        xp_out[0, T - 16 :, lanes(p)] = jnp.where(at_end, tail + more, tail).astype(BF16)

    for stream, step in ((2, 0), (0, 1), (3, 0), (1, 1)):
        advance(stream, step)
    dh_finish(0)
    dh_start(1)
    loop(steps, x_grads)
    vec_start(0)
    store(xr_out, xr_hbm_out)
    for stream, step in ((2, 1), (0, 2), (3, 1), (1, 2)):
        advance(stream, step)
    dh_finish(1)
    dh_start(2)
    vec_finish(0)
    vec_start(1)
    for stream, step in ((2, 2), (0, 3), (3, 2), (1, 3)):
        advance(stream, step)
    vec_finish(1)
    vec_start(2)
    dh_finish(2)
    late = dh_land[first_ref[0, me]] + dh_land[last_ref[0, me]]
    loop(steps, functools.partial(x_tail, jnp.broadcast_to(late, (8, RANK))))
    store(xp_out, xp_hbm_out)
    for stream, step in ((2, 3), (0, 4), (3, 3), (1, 4)):
        advance(stream, step)
    vec_finish(2)
    store(vec_out, vec_hbm_out)
    for stream, step in ((2, 4), (0, 5), (3, 4), (1, 5), (2, 5), (3, 5)):
        advance(stream, step)

    for view, sem in pending:
        bulk_wait(view, sem)
    for copy in stores:
        copy.wait()


def results(pairs, *refs):
    sources, outs, held, (in_sem, out_sem) = refs[:6], refs[6:15], refs[15:21], refs[21:]
    loads = [
        pltpu.make_async_copy(a, b, in_sem.at[n]) for n, (a, b) in enumerate(zip(sources, held))
    ]
    for load in loads:
        load.start()
    moves = [[(held[n], outs[n])] for n in range(4)]
    moves.append([(held[4].at[pl.ds(pairs * LANES, pairs * LANES)], outs[4])])
    for p in range(pairs):
        lanes = pl.ds(p * LANES, LANES)
        moves[4].append((held[4].at[lanes], outs[5].at[:, lanes]))
    moves.append([(held[5].at[n], outs[6 + n]) for n in range(3)])
    copies = []
    for load, group in zip(loads, moves):
        load.wait()
        for src, dst in group:
            copies.append(pltpu.make_async_copy(src, dst, out_sem.at[len(copies)]))
            copies[-1].start()
    for copy in copies:
        copy.wait()


def per_device(
    query_text_memory,
    query_text_feed,
    reply_acceptor_memory,
    reply_feed,
    reply_cotangent_vector,
    query_placement,
    reply_parent_query,
    fading_narrowing,
    fading_widening,
    fading_anchor_rate,
    self_emphasis,
    lagged_token_fraction,
):
    devices = lax.axis_size("dp")
    ranks = lax.axis_size("mp")
    channels = query_text_feed.shape[2]
    pairs = channels // LANES
    per = HEAD * pairs // devices
    stages = stages_of(devices)
    size = [channels // 2]
    for g, n in stages:
        size.append(size[-1] // n)

    def vmem(*shape, dtype=F32):
        return pltpu.VMEM(shape, dtype)

    operands = (
        query_placement[None],
        reply_parent_query[None],
        query_text_memory,
        query_text_feed,
        reply_acceptor_memory,
        reply_feed,
        reply_cotangent_vector,
        fading_narrowing,
        fading_widening,
        fading_anchor_rate[None],
        self_emphasis[None],
        lagged_token_fraction[None],
    )
    dma = pltpu.SemaphoreType.DMA
    shapes = [
        jax.ShapeDtypeStruct(a.shape, BF16)
        for a in (reply_acceptor_memory, reply_feed, query_text_memory, query_text_feed)
    ]
    scratch = [pltpu.VMEM(a.shape, a.dtype) for a in shapes]
    scratch += [vmem(3, 1, channels)]
    scratch += [pltpu.VMEM(a.shape, a.dtype) for a in operands]
    scratch += [
        vmem(1, 2 * devices, dtype=jnp.int32),
        vmem(1, devices, dtype=jnp.int32),
        vmem(1, devices, dtype=jnp.int32),
        pltpu.SMEM((1, 2 * devices), jnp.int32),
        pltpu.SMEM((1, devices), jnp.int32),
        pltpu.SMEM((1, devices), jnp.int32),
        vmem(len(LEVELS) * T, T, dtype=BF16),
        vmem(T, len(LEVELS) * T, dtype=BF16),
        vmem(len(LEVELS) * T, min(2 * LANES, channels)),
        vmem(1, channels),
        vmem(devices, 1, channels),
        vmem(3 * T, channels),
        vmem(T, RANK),
        vmem(ranks, T, RANK),
        vmem(2 * T, RANK),
        vmem(ranks, 2 * T, RANK),
        vmem(8, channels),
        vmem(8, RANK),
        vmem(ranks, 8, RANK),
        vmem(3 * T, channels),
        vmem(3 * T, channels),
        vmem(devices, per, LANES),
        vmem(devices, per, LANES),
        vmem(devices, 2, per, LANES),
        vmem(2 * devices, per, LANES),
        vmem(devices, 2, per, LANES),
        vmem(devices, 2, per, LANES),
        vmem(devices, per, LANES),
        vmem(devices, per, LANES),
        vmem(2, T, channels),
        vmem(2, T, channels),
        vmem(3 * T, RANK),
        vmem(3 * T, channels),
        vmem(2 * T, RANK),
        vmem(ranks, 2 * T, RANK),
        vmem(T, RANK),
        vmem(ranks, T, RANK),
        vmem(3 * T, RANK),
        vmem(2 * devices, 1, RANK),
        vmem(16, channels),
        vmem(9, 1, channels),
        vmem(sum(n for _, n in stages), 3, 1, channels),
        vmem(2 * channels, RANK),
        vmem(4, size[1], RANK),
        vmem(4, size[2], RANK),
        vmem(4, size[3], RANK),
        vmem(4, stages[0][1], size[1], RANK),
        vmem(4, stages[1][1], size[2], RANK),
        vmem(4, stages[2][1], size[3], RANK),
        vmem(2 * channels, RANK),
        dma((len(operands),)),
        dma((3,)),
        dma((9,)),
        dma,
        dma,
        dma((ranks,)),
        dma((ranks,)),
        dma((ranks,)),
        dma((ranks,)),
        dma((ranks,)),
        dma((ranks,)),
        dma((4,)),
        dma((4,)),
        dma((ranks,)),
        dma((ranks,)),
        dma((ranks,)),
        dma((ranks,)),
        dma((3, 8)),
        dma((3, 8)),
        dma((3, 8)),
        dma((3, 8)),
        dma((4, 3, 8)),
        dma((4, 3, 8)),
        dma((4, 3, 8)),
        dma((4, 3, 8)),
    ]
    far = pl.BlockSpec(memory_space=pltpu.HBM)
    moved = pl.pallas_call(
        functools.partial(body, devices, ranks, channels),
        out_shape=(
            *shapes,
            jax.ShapeDtypeStruct((2 * channels, RANK), F32),
            jax.ShapeDtypeStruct((3, 1, channels), F32),
        ),
        in_specs=[far] * len(operands),
        out_specs=[far] * 6,
        scratch_shapes=scratch,
        compiler_params=pltpu.CompilerParams(
            collective_id=0, has_side_effects=True, vmem_limit_bytes=VMEM
        ),
    )(*operands)
    rkv, xr, kv, xp, down, up, *vectors = pl.pallas_call(
        functools.partial(results, pairs),
        out_shape=(
            *shapes,
            jax.ShapeDtypeStruct(fading_narrowing.shape, F32),
            jax.ShapeDtypeStruct(fading_widening.shape, F32),
            *[jax.ShapeDtypeStruct((1, channels), F32)] * 3,
        ),
        in_specs=[far] * 6,
        out_specs=[far] * 9,
        scratch_shapes=[pltpu.VMEM(a.shape, a.dtype) for a in moved]
        + [dma((6,)), dma((8 + pairs,))],
        compiler_params=pltpu.CompilerParams(vmem_limit_bytes=VMEM),
    )(*moved)
    return rkv, xr, kv, xp, down, up, *[v.reshape(channels) for v in vectors]


def solution(mesh):
    in_specs = (
        P(None, "dp", None, "mp"),
        P("dp", None, "mp"),
        P(None, "dp", None, "mp"),
        P("dp", None, "mp"),
        P("dp", None, "mp"),
        P(),
        P(),
        P("mp", None),
        P(None, "mp"),
        P("mp"),
        P("mp"),
        P("mp"),
    )
    out_specs = (
        P(None, "dp", None, "mp"),
        P("dp", None, "mp"),
        P(None, "dp", None, "mp"),
        P("dp", None, "mp"),
        P("mp", None),
        P(None, "mp"),
        P("mp"),
        P("mp"),
        P("mp"),
    )
    return jax.shard_map(
        per_device, mesh=mesh, in_specs=in_specs, out_specs=out_specs, check_vma=False
    )
```

time: 111 us -> 101 us (0.910)
  Pallas kernels: 108 us -> 101 us
    pallas_call x1, Pallas kernels: 106 us -> 97.7 us  [per_device(): pl.pallas_call(functools.partial(body, devices, ranks, channels), out_sha...]
where the time goes in v3:
time: 101 us
  Pallas kernels  101 us (100%)
    pallas_call x1, Pallas kernels, per_device(): pl.pallas_call(functools.partial(body, devices, ranks, channels), out_sha...  97.7 us
    pallas_call x1, Pallas kernels, per_device(): pl.pallas_call(functools.partial(results, pairs), out_shape=(*shapes, jax...  2.81 us

profile of v3, /device:TPU:1, one launch (start us, length us, event | category | flops | bytes accessed | tf_op | source)
XLA Modules:
  0.0 101.2 jit_solution(9206885343993011142)
XLA Ops:
  0.6 97.7 %shard_map.187 = (bf16[3,2,64,1024]{3,2,1,0:T(8,128)(2,1)}, bf16[2,64,1024]{2,1,0:T(8,128)(2,1)}, bf16[2,1,64,1024]{3,2,1,0:T(8,128)(2,1)}, bf16[1,64,1024]{2,1,...) custom-call(s32[1,64]{1,0:T(1,128)} %bitcast.11, s32[1,128]{1,0:T(1,128)} %bitcast.12, ...), custom_call_target="tpu_custom_call" | custom-call | tf_op jit(solution)/shard_map/pallas_call | solution.py:911
  98.4 2.8 %shard_map.188 = (bf16[3,2,64,1024]{3,2,1,0:T(8,128)(2,1)}, bf16[2,64,1024]{2,1,0:T(8,128)(2,1)}, bf16[2,1,64,1024]{3,2,1,0:T(8,128)(2,1)}, bf16[1,64,1024]{2,1,...) custom-call(bf16[3,2,64,1024]{3,2,1,0:T(8,128)(2,1)} %get-tuple-elem, ...), custom_call_target="tpu_custom_call" | custom-call | tf_op jit(solution)/shard_map/pallas_call | solution.py:925

commit v4 on v3

--- a/solution.py
+++ b/solution.py
@@ -202,6 +202,8 @@
     stages = stages_of(devices)
 
     def lanes(p):
+        if isinstance(p, int):
+            return pl.ds(p * wide, wide)
         return pl.ds(pl.multiple_of(p * wide, LANES), wide)
 
     rows_of = lanes
@@ -211,6 +213,16 @@
             lax.fori_loop(0, n, lambda i, c: (fn(i), c)[1], 0)
             return None
         return lax.fori_loop(0, n, fn, init)
+
+    def unrolled(n, fn, init=None):
+        for i in range(n):
+            init = fn(i) if init is None else fn(i, init)
+        return init
+
+    def by_two(n, fn):
+        if n % 2:
+            return loop(n, fn)
+        return loop(n // 2, lambda i: (fn(2 * i), fn(2 * i + 1)))
 
     def remote(src, dst, ssem, rsem, axis, peer):
         return pltpu.make_async_remote_copy(
@@ -226,6 +238,13 @@
         pltpu.make_async_copy(view, view, sem).wait()
 
     pending = []
+    settled = [0]
+
+    def settle():
+        for view, sem in pending[: settled[0]]:
+            bulk_wait(view, sem)
+        del pending[: settled[0]]
+        settled[0] = len(pending)
 
     barrier = pltpu.get_barrier_semaphore()
 
@@ -289,11 +308,37 @@
     for fetch in fetches[:4]:
         fetch.wait()
     row_src[...] = xp_ref[0, T - 16 :, :].astype(F32)[15:16]
-    partial = loop(steps, mix, jnp.zeros((3 * T, RANK), F32))
+    partial = unrolled(steps, mix, jnp.zeros((3 * T, RANK), F32))
     hid_p[...] = partial[:T]
     hid_r[...] = partial[T:]
     for fetch in fetches[4:]:
         fetch.wait()
+    def column(row):
+        n = row.shape[1]
+        diagonal = lax.broadcasted_iota(jnp.int32, (n, n), 0) == lax.broadcasted_iota(
+            jnp.int32, (n, n), 1
+        )
+        return jnp.sum(jnp.where(diagonal, row, 0), axis=1, keepdims=True)
+
+    placed, parents = place_ref[...], parent_ref[...]
+    pairs_at = (devices, 2 * devices)
+    match = column(placed) == parents
+    slot = lax.broadcasted_iota(jnp.int32, pairs_at, 0)
+    owner_vec[...] = jnp.max(jnp.where(match, slot, 0), axis=0, keepdims=True)
+    match = column(parents) == placed
+    response = lax.broadcasted_iota(jnp.int32, pairs_at[::-1], 0)
+    first_vec[...] = jnp.min(
+        jnp.where(match, response, 2 * devices - 1), axis=0, keepdims=True
+    )
+    last_vec[...] = jnp.max(jnp.where(match, response, 0), axis=0, keepdims=True)
+    indices = [
+        pltpu.make_async_copy(src, dst, index_sem.at[n])
+        for n, (src, dst) in enumerate(
+            ((owner_vec, owner_ref), (first_vec, first_ref), (last_vec, last_ref))
+        )
+    ]
+    for copy in indices:
+        copy.start()
     pl.semaphore_wait(barrier, devices - 1 + ranks - 1)
 
     def exchange(src, land, ssem, rsem):
@@ -317,10 +362,10 @@
         remote(row_src, row_land.at[me], row_s, row_r, "dp", peer).start()
 
     exchange(hid_p, hid_p_land, hid_p_s, hid_p_r)
+    exchange(hid_r, hid_r_land, hid_r_s, hid_r_r)
     loop(devices - 1, send_row)
     pending.append((row_land.at[pl.ds(0, devices - 1)], row_s))
     row_land[me] = row_src[...]
-    exchange(hid_r, hid_r_land, hid_r_s, hid_r_r)
     t_sq = lax.broadcasted_iota(jnp.int32, (T, T), 0)
     j_sq = lax.broadcasted_iota(jnp.int32, (T, T), 1)
     before = (j_sq < t_sq).astype(F32).astype(BF16)
@@ -359,34 +404,46 @@
         loop(devices - 1, send)
         pending.append((src.at[pl.ds(0, devices - 1)], route_s.at[n]))
 
-    def column(row):
-        n = row.shape[1]
-        diagonal = lax.broadcasted_iota(jnp.int32, (n, n), 0) == lax.broadcasted_iota(
-            jnp.int32, (n, n), 1
-        )
-        return jnp.sum(jnp.where(diagonal, row, 0), axis=1, keepdims=True)
-
-    placed, parents = place_ref[...], parent_ref[...]
-    pairs_at = (devices, 2 * devices)
-    match = column(placed) == parents
-    slot = lax.broadcasted_iota(jnp.int32, pairs_at, 0)
-    owner_vec[...] = jnp.max(jnp.where(match, slot, 0), axis=0, keepdims=True)
-    match = column(parents) == placed
-    response = lax.broadcasted_iota(jnp.int32, pairs_at[::-1], 0)
-    first_vec[...] = jnp.min(
-        jnp.where(match, response, 2 * devices - 1), axis=0, keepdims=True
-    )
-    last_vec[...] = jnp.max(jnp.where(match, response, 0), axis=0, keepdims=True)
-    indices = [
-        pltpu.make_async_copy(src, dst, index_sem.at[n])
-        for n, (src, dst) in enumerate(
-            ((owner_vec, owner_ref), (first_vec, first_ref), (last_vec, last_ref))
-        )
-    ]
-    for copy in indices:
-        copy.start()
+    th_ref[:T, :] = jnp.tanh(exchanged(hid_p_land, hid_p_r))
+    unrolled(steps, functools.partial(decays, 0, 1))
+    route(0, send_f1, lambda m: recv_f1.at[m])
+    recv_f1[me] = send_f1[me]
+
+    bulk_wait(row_land.at[pl.ds(0, devices - 1)], row_r)
     for copy in indices:
         copy.wait()
+    lead_rows = [row_land[owner_ref[0, 2 * me + i]] for i in range(2)]
+    row8 = lax.broadcasted_iota(jnp.int32, (8, channels), 0)
+    lead[...] = jnp.where(row8 == 0, lead_rows[0], jnp.where(row8 == 1, lead_rows[1], 0.0))
+
+    def lead_mix(p, acc):
+        fl = f_ref[:, lanes(p)] * lead[:, lanes(p)]
+        for i in range(2):
+            at = (i + 1) * T
+            mixed[at : at + 1, lanes(p)] = mixed[at : at + 1, lanes(p)] + fl[i : i + 1]
+        return acc + dot3(nn, split(fl), split(down_ref[rows_of(p), :]))
+
+    lead_hid[...] = unrolled(steps, lead_mix, jnp.zeros((8, RANK), F32))
+    exchange(lead_hid, lead_land, lead_s, lead_r)
+    hidden = exchanged(hid_r_land, hid_r_r)
+    th_ref[T:, :] = jnp.tanh(hidden)
+    extra = exchanged(lead_land, lead_r)
+    for i in range(2):
+        at = (i + 1) * T
+        th_ref[at : at + 1, :] = jnp.tanh(hidden[i * T : i * T + 1] + extra[i : i + 1])
+    unrolled(steps, functools.partial(decays, 1, 3))
+    route(1, send_b1, lambda m: recv_b1.at[pl.ds(2 * m, 2)])
+    recv_b1[pl.ds(2 * me, 2)] = send_b1[me]
+
+    bulk_wait(recv_f1.at[pl.ds(0, devices - 1)], route_r.at[0])
+
+    def shuffle_f(n):
+        send_f2[n, 0] = recv_f1[owner_ref[0, 2 * n]]
+        send_f2[n, 1] = recv_f1[owner_ref[0, 2 * n + 1]]
+
+    loop(devices, shuffle_f)
+    route(2, send_f2, lambda m: recv_f2.at[m])
+    recv_f2[me] = send_f2[me]
 
     def gap_mask(shape, t_axis, level):
         t = lax.broadcasted_iota(jnp.int32, shape, t_axis)
@@ -407,45 +464,6 @@
     apart = t_row ^ s_col
     for level, b in enumerate(LEVELS):
         masks_ref[level * T : (level + 1) * T, :] = ((apart >= b) & (apart < 2 * b)).astype(F32)
-
-    th_ref[:T, :] = jnp.tanh(exchanged(hid_p_land, hid_p_r))
-    loop(steps, functools.partial(decays, 0, 1))
-    bulk_wait(row_land.at[pl.ds(0, devices - 1)], row_r)
-    lead_rows = [row_land[owner_ref[0, 2 * me + i]] for i in range(2)]
-    row8 = lax.broadcasted_iota(jnp.int32, (8, channels), 0)
-    lead[...] = jnp.where(row8 == 0, lead_rows[0], jnp.where(row8 == 1, lead_rows[1], 0.0))
-
-    def lead_mix(p, acc):
-        fl = f_ref[:, lanes(p)] * lead[:, lanes(p)]
-        for i in range(2):
-            at = (i + 1) * T
-            mixed[at : at + 1, lanes(p)] = mixed[at : at + 1, lanes(p)] + fl[i : i + 1]
-        return acc + dot3(nn, split(fl), split(down_ref[rows_of(p), :]))
-
-    lead_hid[...] = loop(steps, lead_mix, jnp.zeros((8, RANK), F32))
-    exchange(lead_hid, lead_land, lead_s, lead_r)
-    route(0, send_f1, lambda m: recv_f1.at[m])
-    recv_f1[me] = send_f1[me]
-
-    hidden = exchanged(hid_r_land, hid_r_r)
-    th_ref[T:, :] = jnp.tanh(hidden)
-    extra = exchanged(lead_land, lead_r)
-    for i in range(2):
-        at = (i + 1) * T
-        th_ref[at : at + 1, :] = jnp.tanh(hidden[i * T : i * T + 1] + extra[i : i + 1])
-    loop(steps, functools.partial(decays, 1, 3))
-    route(1, send_b1, lambda m: recv_b1.at[pl.ds(2 * m, 2)])
-    recv_b1[pl.ds(2 * me, 2)] = send_b1[me]
-
-    bulk_wait(recv_f1.at[pl.ds(0, devices - 1)], route_r.at[0])
-
-    def shuffle_f(n):
-        send_f2[n, 0] = recv_f1[owner_ref[0, 2 * n]]
-        send_f2[n, 1] = recv_f1[owner_ref[0, 2 * n + 1]]
-
-    loop(devices, shuffle_f)
-    route(2, send_f2, lambda m: recv_f2.at[m])
-    recv_f2[me] = send_f2[me]
 
     ones_block = (
         (
@@ -505,7 +523,7 @@
         else:
             vec[1, :, cols] = vec[1, :, cols] + part
 
-    loop(steps, functools.partial(inner, 0))
+    by_two(steps, functools.partial(inner, 0))
     bulk_wait(recv_b1.at[pl.ds(0, 2 * (devices - 1))], route_r.at[1])
 
     def shuffle_b(n):
@@ -514,7 +532,7 @@
     loop(devices, shuffle_b)
     route(3, send_b2, lambda m: recv_b2.at[m])
     recv_b2[me] = send_b2[me]
-    loop(steps, functools.partial(inner, 1))
+    by_two(steps, functools.partial(inner, 1))
 
     def landed(ref, p, *i):
         parts = [
@@ -548,14 +566,14 @@
         return acc + dot3(nt, split(dz_ref[lo * T : hi * T, lanes(p)]), split(up_ref[:, lanes(p)]))
 
     bulk_wait(recv_f2.at[pl.ds(0, devices - 1)], route_r.at[2])
-    loop(steps, outer_r)
-    dth_r_src[...] = loop(
+    unrolled(steps, outer_r)
+    dth_r_src[...] = unrolled(
         steps, functools.partial(dth_part, 1, 3), jnp.zeros((2 * T, RANK), F32)
     )
     exchange(dth_r_src, dth_r_land, dth_r_s, dth_r_r)
     bulk_wait(recv_b2.at[pl.ds(0, devices - 1)], route_r.at[3])
-    loop(steps, outer_p)
-    dth_p_src[...] = loop(steps, functools.partial(dth_part, 0, 1), jnp.zeros((T, RANK), F32))
+    unrolled(steps, outer_p)
+    dth_p_src[...] = unrolled(steps, functools.partial(dth_part, 0, 1), jnp.zeros((T, RANK), F32))
     exchange(dth_p_src, dth_p_land, dth_p_s, dth_p_r)
     store(rkv_out, rkv_hbm_out)
     store(kv_out, kv_hbm_out)
@@ -670,19 +688,19 @@
         dz = dz_ref[:, lanes(p)]
         g = dot3(tn, split(th_ref[...]), split(dz))
         for n in range(blocks):
-            rows = pl.ds(pl.multiple_of(p * wide + n * LANES, LANES), LANES)
+            rows = pl.ds(p * wide + n * LANES, LANES)
             grad[rows, :] = g[:, n * LANES : (n + 1) * LANES]
         vec[0, :, lanes(p)] = jnp.sum(dz, axis=0, keepdims=True)
 
     def down_grads(p):
-        rows = pl.ds(pl.multiple_of(channels + p * wide, LANES), wide)
+        rows = pl.ds(channels + p * wide, wide)
         grad[rows, :] = dot3(tn, split(mixed[:, lanes(p)]), split(dh_ref[...]))
 
     def both_streams(stream, fn):
         half = (steps + 1) // 2
-        loop(half, fn)
+        unrolled(half, fn)
         rs_start(stream, 0)
-        loop(steps - half, lambda p: fn(p + half))
+        unrolled(steps - half, lambda p: fn(p + half))
         rs_start(stream + 1, 0)
 
     both_streams(0, up_grads)
@@ -728,29 +746,36 @@
         advance(stream, step)
     dh_finish(0)
     dh_start(1)
-    loop(steps, x_grads)
+    by_two(steps, x_grads)
     vec_start(0)
     store(xr_out, xr_hbm_out)
+    settle()
     for stream, step in ((2, 1), (0, 2), (3, 1), (1, 2)):
         advance(stream, step)
     dh_finish(1)
     dh_start(2)
     vec_finish(0)
     vec_start(1)
+    settle()
     for stream, step in ((2, 2), (0, 3), (3, 2), (1, 3)):
         advance(stream, step)
     vec_finish(1)
     vec_start(2)
     dh_finish(2)
     late = dh_land[first_ref[0, me]] + dh_land[last_ref[0, me]]
-    loop(steps, functools.partial(x_tail, jnp.broadcast_to(late, (8, RANK))))
+    unrolled(steps, functools.partial(x_tail, jnp.broadcast_to(late, (8, RANK))))
     store(xp_out, xp_hbm_out)
+    settle()
     for stream, step in ((2, 3), (0, 4), (3, 3), (1, 4)):
         advance(stream, step)
     vec_finish(2)
     store(vec_out, vec_hbm_out)
-    for stream, step in ((2, 4), (0, 5), (3, 4), (1, 5), (2, 5), (3, 5)):
+    settle()
+    for stream, step in ((2, 4), (0, 5), (3, 4), (1, 5)):
         advance(stream, step)
+    settle()
+    advance(2, 5)
+    advance(3, 5)
 
     for view, sem in pending:
         bulk_wait(view, sem)

time: 101 us -> 98.4 us (0.974)
  Pallas kernels: 101 us -> 97.6 us
    pallas_call x1, Pallas kernels: 97.7 us -> 94.8 us  [per_device(): pl.pallas_call(functools.partial(body, devices, ranks, channels), out_sha...]
where the time goes in v4:
time: 98.4 us; the launch traced here: 98.3 us
  Pallas kernels  97.6 us (99%)
    pallas_call x1, Pallas kernels, per_device(): pl.pallas_call(functools.partial(body, devices, ranks, channels), out_sha...  94.8 us
    pallas_call x1, Pallas kernels, per_device(): pl.pallas_call(functools.partial(results, pairs), out_shape=(*shapes, jax...  2.81 us

profile of v4, /device:TPU:1, one launch (start us, length us, event | category | flops | bytes accessed | tf_op | source)
XLA Modules:
  0.0 98.3 jit_solution(13737090677005000063)
XLA Ops:
  0.6 94.8 %shard_map.187 = (bf16[3,2,64,1024]{3,2,1,0:T(8,128)(2,1)}, bf16[2,64,1024]{2,1,0:T(8,128)(2,1)}, bf16[2,1,64,1024]{3,2,1,0:T(8,128)(2,1)}, bf16[1,64,1024]{2,1,...) custom-call(s32[1,64]{1,0:T(1,128)} %bitcast.11, s32[1,128]{1,0:T(1,128)} %bitcast.12, ...), custom_call_target="tpu_custom_call" | custom-call | tf_op jit(solution)/shard_map/pallas_call | solution.py:936
  95.5 2.8 %shard_map.188 = (bf16[3,2,64,1024]{3,2,1,0:T(8,128)(2,1)}, bf16[2,64,1024]{2,1,0:T(8,128)(2,1)}, bf16[2,1,64,1024]{3,2,1,0:T(8,128)(2,1)}, bf16[1,64,1024]{2,1,...) custom-call(bf16[3,2,64,1024]{3,2,1,0:T(8,128)(2,1)} %get-tuple-elem, ...), custom_call_target="tpu_custom_call" | custom-call | tf_op jit(solution)/shard_map/pallas_call | solution.py:950

commit v5 on v4

--- a/solution.py
+++ b/solution.py
@@ -234,6 +234,10 @@
             device_id_type=MESH,
         )
 
+    def nth_peer(i):
+        k = (i + 1) // 2
+        return lax.rem(me + devices // 2 + k * (1 - 2 * (i % 2)), devices)
+
     def bulk_wait(view, sem):
         pltpu.make_async_copy(view, view, sem).wait()
 
@@ -358,7 +362,7 @@
         return total
 
     def send_row(i):
-        peer = lax.rem(me + 1 + i, devices)
+        peer = nth_peer(i)
         remote(row_src, row_land.at[me], row_s, row_r, "dp", peer).start()
 
     exchange(hid_p, hid_p_land, hid_p_s, hid_p_r)
@@ -396,9 +400,11 @@
                 else:
                     send_b1[at, i - 1] = part
 
-    def route(n, src, dst_of):
+    def route(n, src, dst_of, fill=None):
         def send(i):
-            peer = lax.rem(me + 1 + i, devices)
+            peer = nth_peer(i)
+            if fill is not None:
+                fill(peer)
             remote(src.at[peer], dst_of(me), route_s.at[n], route_r.at[n], "dp", peer).start()
 
         loop(devices - 1, send)
@@ -441,8 +447,8 @@
         send_f2[n, 0] = recv_f1[owner_ref[0, 2 * n]]
         send_f2[n, 1] = recv_f1[owner_ref[0, 2 * n + 1]]
 
-    loop(devices, shuffle_f)
-    route(2, send_f2, lambda m: recv_f2.at[m])
+    route(2, send_f2, lambda m: recv_f2.at[m], shuffle_f)
+    shuffle_f(me)
     recv_f2[me] = send_f2[me]
 
     def gap_mask(shape, t_axis, level):
@@ -523,16 +529,16 @@
         else:
             vec[1, :, cols] = vec[1, :, cols] + part
 
-    by_two(steps, functools.partial(inner, 0))
+    loop(steps, functools.partial(inner, 0))
     bulk_wait(recv_b1.at[pl.ds(0, 2 * (devices - 1))], route_r.at[1])
 
     def shuffle_b(n):
         send_b2[n] = recv_b1[first_ref[0, n]] + recv_b1[last_ref[0, n]]
 
-    loop(devices, shuffle_b)
-    route(3, send_b2, lambda m: recv_b2.at[m])
+    route(3, send_b2, lambda m: recv_b2.at[m], shuffle_b)
+    shuffle_b(me)
     recv_b2[me] = send_b2[me]
-    by_two(steps, functools.partial(inner, 1))
+    loop(steps, functools.partial(inner, 1))
 
     def landed(ref, p, *i):
         parts = [
@@ -692,9 +698,17 @@
             grad[rows, :] = g[:, n * LANES : (n + 1) * LANES]
         vec[0, :, lanes(p)] = jnp.sum(dz, axis=0, keepdims=True)
 
+    def down_of(p, lo, hi):
+        return dot3(
+            tn, split(mixed[lo * T : hi * T, lanes(p)]), split(dh_ref[lo * T : hi * T, :])
+        )
+
+    def down_early(p):
+        grad[pl.ds(channels + p * wide, wide), :] = down_of(p, 1, 3)
+
     def down_grads(p):
         rows = pl.ds(channels + p * wide, wide)
-        grad[rows, :] = dot3(tn, split(mixed[:, lanes(p)]), split(dh_ref[...]))
+        grad[rows, :] = grad[rows, :] + down_of(p, 0, 1)
 
     def both_streams(stream, fn):
         half = (steps + 1) // 2
@@ -712,6 +726,7 @@
     dh_start(0)
     advance(0, 0)
     advance(1, 0)
+    unrolled(steps, down_early)
     th = th_ref[:T, :]
     dh_ref[:T, :] = exchanged(dth_p_land, dth_p_r) * (1.0 - th * th)
     both_streams(2, down_grads)
@@ -746,7 +761,7 @@
         advance(stream, step)
     dh_finish(0)
     dh_start(1)
-    by_two(steps, x_grads)
+    loop(steps, x_grads)
     vec_start(0)
     store(xr_out, xr_hbm_out)
     settle()

time: 98.4 us -> 97.3 us (0.989)
  Pallas kernels: 97.6 us -> 96.5 us
    pallas_call x1, Pallas kernels: 94.8 us -> 93.7 us  [per_device(): pl.pallas_call(functools.partial(body, devices, ranks, channels), out_sha...]
where the time goes in v5:
time: 97.3 us; the launch traced here: 97.2 us
  Pallas kernels  96.5 us (99%)
    pallas_call x1, Pallas kernels, per_device(): pl.pallas_call(functools.partial(body, devices, ranks, channels), out_sha...  93.7 us
    pallas_call x1, Pallas kernels, per_device(): pl.pallas_call(functools.partial(results, pairs), out_shape=(*shapes, jax...  2.81 us

profile of v5, /device:TPU:1, one launch (start us, length us, event | category | flops | bytes accessed | tf_op | source)
XLA Modules:
  0.0 97.2 jit_solution(3405699022932144409)
XLA Ops:
  0.6 93.7 %shard_map.187 = (bf16[3,2,64,1024]{3,2,1,0:T(8,128)(2,1)}, bf16[2,64,1024]{2,1,0:T(8,128)(2,1)}, bf16[2,1,64,1024]{3,2,1,0:T(8,128)(2,1)}, bf16[1,64,1024]{2,1,...) custom-call(s32[1,64]{1,0:T(1,128)} %bitcast.11, s32[1,128]{1,0:T(1,128)} %bitcast.12, ...), custom_call_target="tpu_custom_call" | custom-call | tf_op jit(solution)/shard_map/pallas_call | solution.py:951
  94.4 2.8 %shard_map.188 = (bf16[3,2,64,1024]{3,2,1,0:T(8,128)(2,1)}, bf16[2,64,1024]{2,1,0:T(8,128)(2,1)}, bf16[2,1,64,1024]{3,2,1,0:T(8,128)(2,1)}, bf16[1,64,1024]{2,1,...) custom-call(bf16[3,2,64,1024]{3,2,1,0:T(8,128)(2,1)} %get-tuple-elem, ...), custom_call_target="tpu_custom_call" | custom-call | tf_op jit(solution)/shard_map/pallas_call | solution.py:965
